TPU v7x, 512 devices: a whole 4x8x8 slice. The times are simulated.
512 devices in a mesh: rows: 16 (over x, z_hi), cols: 32 (over z_lo, y, core).
Axes of the slice: x: 4, y: 8, z: 8 (z_hi: 4, z_lo: 2; z = z_hi * 2 + z_lo), core: 2. Of those that a mesh axis runs over, the one named last changes fastest.
Arguments:
- coefficients: float32 [1024, 8192], P('cols', 'rows'), may hold values from -6 to 6
- factor_panel: float32 [8192, 1024], P('rows'), may hold values from -0.0625 to 0.0625
- block_inverse: float32 [8192, 512], P('rows'), may hold values from -0.044194174 to 2, as said below
- train_inputs: float32 [14, 8192], P(None, 'rows'), may hold values from 0 to 1
- query_points: float32 [14, 8192], replicated, may hold values from 0 to 1
- inv_length: float32 [14], replicated, may hold values from 0.25 to 2
- amplitude: float32 [1024], P('cols'), may hold values from 0.02 to 0.2
Outputs:
- weights: float32 [1024, 8192], P('cols', 'rows')
- predicted_mean: float32 [1024, 8192], P('cols', 'rows')
Inputs may be any that keep to these rules, and one draw needn't show every extreme that they name: `block_inverse`: each block of 512 rows is lower triangular, with diagonal entries from 1 to 2.
All inputs are finite; a program needn't handle non-finite values.
Results may differ from a plain program's by a relative error of at most 0.004.
Values may be sent and summed in bfloat16 or wider, within the bound.
No kernel may reach another device: no remote copies, remote signals or barrier semaphores. Data moves between devices by JAX's collectives and lax.ppermute only.
A program may use at most 64 MiB of HBM per device.

v0:
```python
import jax
import jax.numpy as jnp
from jax import lax
from jax.sharding import PartitionSpec as P


def kernel_values(train_part, query_part, inv_length):
    squared = jnp.zeros((train_part.shape[1], query_part.shape[1]), jnp.float32)
    for dim_index in range(train_part.shape[0]):
        offset = (train_part[dim_index][:, None] - query_part[dim_index][None, :]) * inv_length[
            dim_index
        ]
        squared = squared + offset * offset
    return jnp.exp(-jnp.sqrt(squared + 1e-06)).astype(jnp.bfloat16)


def solve_product(left, right):
    return jnp.dot(left, right, precision=lax.Precision.HIGHEST, preferred_element_type=jnp.float32)


def on_device(
    coefficients, factor_panel, block_inverse, train_inputs, query_points, inv_length, amplitude
):
    block_len = coefficients.shape[1]
    row_index = lax.axis_index("rows")
    row_count = lax.axis_size("rows")
    solved_block = row_index >= 2
    factor_zero = factor_panel[:, :block_len]
    factor_one = factor_panel[:, block_len:]
    local_one = jnp.where(solved_block, solve_product(coefficients, factor_one), 0.0)
    local_zero = jnp.where(solved_block, solve_product(coefficients, factor_zero), 0.0)
    rest_one = lax.psum(local_one, "rows")
    weights_one = solve_product(coefficients - rest_one, block_inverse)
    carried = jnp.where(row_index == 1, solve_product(weights_one, factor_zero), local_zero)
    rest_zero = lax.psum(carried, "rows")
    weights_zero = solve_product(coefficients - rest_zero, block_inverse)
    weights = jnp.where(
        row_index == 0, weights_zero, jnp.where(row_index == 1, weights_one, coefficients)
    )
    weights_low = weights.astype(jnp.bfloat16)
    piece_len = query_points.shape[1] // row_count

    def single_piece(piece_index):
        chosen = lax.dynamic_slice_in_dim(query_points, piece_index * piece_len, piece_len, 1)
        return jnp.dot(
            weights_low,
            kernel_values(train_inputs, chosen, inv_length),
            preferred_element_type=jnp.float32,
        )

    summed = lax.psum_scatter(
        lax.map(single_piece, jnp.arange(1 * lax.axis_size("rows"), dtype=jnp.int32)),
        "rows",
        scatter_dimension=0,
        tiled=True,
    )
    predicted_mean = summed[0] * amplitude[:, None]
    return (weights, predicted_mean)


def solution(mesh):
    return jax.shard_map(
        on_device,
        mesh=mesh,
        in_specs=(
            P("cols", "rows"),
            P("rows", None),
            P("rows", None),
            P(None, "rows"),
            P(),
            P(),
            P("cols"),
        ),
        out_specs=(P("cols", "rows"), P("cols", "rows")),
        check_vma=False,
    )
```

profile of v0, /device:TPU:8, one launch (start us, length us, event | category | flops | bytes accessed | tf_op | source)
XLA Modules:
  0.0 679.7 jit_solution(9517215299891742110)
XLA Ops:
  7.3 2.7 convolution_select_fusion.2
  10.1 166.2 %all-reduce.3.cloned.1.call-done = f32[32,512]{1,0:T(8,128)} async-done(((f32[32,512]{1,0:T(8,128)}), f32[32,512]{1,0:T(8,128)}) %all-reduce.3.cloned.1.call-update) | async-done | bytes 65552 | tf_op jit(solution)/shard_map/psum | solution.py:32
  176.3 1.6 fusion.51
  180.1 155.7 %all-reduce.5.cloned.1.call-done = f32[32,512]{1,0:T(8,128)} async-done(((f32[32,512]{1,0:T(8,128)}), f32[32,512]{1,0:T(8,128)}) %all-reduce.5.cloned.1.call-update) | async-done | bytes 65552 | tf_op jit(solution)/shard_map/psum | solution.py:35
  335.8 2.2 fusion.55
  338.0 245.5 %while.10 = (s32[]{:T(128)}, f32[16,32,512]{2,1,0:T(8,128)}, f32[14,512]{1,0:T(8,128)S(1)}, s32[16]{0:T(128)S(1)}, f32[14,8192]{1,0:T(8,128)}, /*index=5*/f32[14...) while((s32[]{:T(128)}, f32[16,32,512]{2,1,0:T(8,128)}, ...), condition=%wide.region_3.4_spmd, body=%wide.region_2.3_spmd.sunk | while | flops 31981588 | bytes 278611 | solution.py:52
  341.3 12.1 %fusion.69 = f32[16,32,512]{2,1,0:T(8,128)} fusion(f32[16,32,512]{2,1,0:T(8,128)} %get-tuple-element.250, s32[]{:T(128)} %get-tuple-element.249, bf16[32,512]{1,0:T(8,128)(2,1)S(1)} %get-tuple-element.279, f32[]{:T(128)} %bitcast.104, f32[512]{0:T(512)S(1)} %bitcast.160, f32[512]{0:T(512)S(1)} %bitcast.162, f32[]{:T(128)} %bitcast.108, ...), kind=kOutput, calls=%fused_computation.1.clone.1 | convolution fusion | flops 31981568 | bytes 163328 | tf_op jit(solution)/shard_map/while/body/eval_jaxpr/dot_general | solution.py:45
  356.6 12.1 %fusion.69 = f32[16,32,512]{2,1,0:T(8,128)} fusion(f32[16,32,512]{2,1,0:T(8,128)} %get-tuple-element.250, s32[]{:T(128)} %get-tuple-element.249, bf16[32,512]{1,0:T(8,128)(2,1)S(1)} %get-tuple-element.279, f32[]{:T(128)} %bitcast.104, f32[512]{0:T(512)S(1)} %bitcast.160, f32[512]{0:T(512)S(1)} %bitcast.162, f32[]{:T(128)} %bitcast.108, ...), kind=kOutput, calls=%fused_computation.1.clone.1 | convolution fusion | flops 31981568 | bytes 163328 | tf_op jit(solution)/shard_map/while/body/eval_jaxpr/dot_general | solution.py:45
  372.0 12.1 %fusion.69 = f32[16,32,512]{2,1,0:T(8,128)} fusion(f32[16,32,512]{2,1,0:T(8,128)} %get-tuple-element.250, s32[]{:T(128)} %get-tuple-element.249, bf16[32,512]{1,0:T(8,128)(2,1)S(1)} %get-tuple-element.279, f32[]{:T(128)} %bitcast.104, f32[512]{0:T(512)S(1)} %bitcast.160, f32[512]{0:T(512)S(1)} %bitcast.162, f32[]{:T(128)} %bitcast.108, ...), kind=kOutput, calls=%fused_computation.1.clone.1 | convolution fusion | flops 31981568 | bytes 163328 | tf_op jit(solution)/shard_map/while/body/eval_jaxpr/dot_general | solution.py:45
  387.3 12.1 %fusion.69 = f32[16,32,512]{2,1,0:T(8,128)} fusion(f32[16,32,512]{2,1,0:T(8,128)} %get-tuple-element.250, s32[]{:T(128)} %get-tuple-element.249, bf16[32,512]{1,0:T(8,128)(2,1)S(1)} %get-tuple-element.279, f32[]{:T(128)} %bitcast.104, f32[512]{0:T(512)S(1)} %bitcast.160, f32[512]{0:T(512)S(1)} %bitcast.162, f32[]{:T(128)} %bitcast.108, ...), kind=kOutput, calls=%fused_computation.1.clone.1 | convolution fusion | flops 31981568 | bytes 163328 | tf_op jit(solution)/shard_map/while/body/eval_jaxpr/dot_general | solution.py:45
  402.7 12.1 %fusion.69 = f32[16,32,512]{2,1,0:T(8,128)} fusion(f32[16,32,512]{2,1,0:T(8,128)} %get-tuple-element.250, s32[]{:T(128)} %get-tuple-element.249, bf16[32,512]{1,0:T(8,128)(2,1)S(1)} %get-tuple-element.279, f32[]{:T(128)} %bitcast.104, f32[512]{0:T(512)S(1)} %bitcast.160, f32[512]{0:T(512)S(1)} %bitcast.162, f32[]{:T(128)} %bitcast.108, ...), kind=kOutput, calls=%fused_computation.1.clone.1 | convolution fusion | flops 31981568 | bytes 163328 | tf_op jit(solution)/shard_map/while/body/eval_jaxpr/dot_general | solution.py:45
  418.0 12.1 %fusion.69 = f32[16,32,512]{2,1,0:T(8,128)} fusion(f32[16,32,512]{2,1,0:T(8,128)} %get-tuple-element.250, s32[]{:T(128)} %get-tuple-element.249, bf16[32,512]{1,0:T(8,128)(2,1)S(1)} %get-tuple-element.279, f32[]{:T(128)} %bitcast.104, f32[512]{0:T(512)S(1)} %bitcast.160, f32[512]{0:T(512)S(1)} %bitcast.162, f32[]{:T(128)} %bitcast.108, ...), kind=kOutput, calls=%fused_computation.1.clone.1 | convolution fusion | flops 31981568 | bytes 163328 | tf_op jit(solution)/shard_map/while/body/eval_jaxpr/dot_general | solution.py:45
  433.4 12.1 %fusion.69 = f32[16,32,512]{2,1,0:T(8,128)} fusion(f32[16,32,512]{2,1,0:T(8,128)} %get-tuple-element.250, s32[]{:T(128)} %get-tuple-element.249, bf16[32,512]{1,0:T(8,128)(2,1)S(1)} %get-tuple-element.279, f32[]{:T(128)} %bitcast.104, f32[512]{0:T(512)S(1)} %bitcast.160, f32[512]{0:T(512)S(1)} %bitcast.162, f32[]{:T(128)} %bitcast.108, ...), kind=kOutput, calls=%fused_computation.1.clone.1 | convolution fusion | flops 31981568 | bytes 163328 | tf_op jit(solution)/shard_map/while/body/eval_jaxpr/dot_general | solution.py:45
  448.7 12.1 %fusion.69 = f32[16,32,512]{2,1,0:T(8,128)} fusion(f32[16,32,512]{2,1,0:T(8,128)} %get-tuple-element.250, s32[]{:T(128)} %get-tuple-element.249, bf16[32,512]{1,0:T(8,128)(2,1)S(1)} %get-tuple-element.279, f32[]{:T(128)} %bitcast.104, f32[512]{0:T(512)S(1)} %bitcast.160, f32[512]{0:T(512)S(1)} %bitcast.162, f32[]{:T(128)} %bitcast.108, ...), kind=kOutput, calls=%fused_computation.1.clone.1 | convolution fusion | flops 31981568 | bytes 163328 | tf_op jit(solution)/shard_map/while/body/eval_jaxpr/dot_general | solution.py:45
  464.1 12.1 %fusion.69 = f32[16,32,512]{2,1,0:T(8,128)} fusion(f32[16,32,512]{2,1,0:T(8,128)} %get-tuple-element.250, s32[]{:T(128)} %get-tuple-element.249, bf16[32,512]{1,0:T(8,128)(2,1)S(1)} %get-tuple-element.279, f32[]{:T(128)} %bitcast.104, f32[512]{0:T(512)S(1)} %bitcast.160, f32[512]{0:T(512)S(1)} %bitcast.162, f32[]{:T(128)} %bitcast.108, ...), kind=kOutput, calls=%fused_computation.1.clone.1 | convolution fusion | flops 31981568 | bytes 163328 | tf_op jit(solution)/shard_map/while/body/eval_jaxpr/dot_general | solution.py:45
  479.4 12.1 %fusion.69 = f32[16,32,512]{2,1,0:T(8,128)} fusion(f32[16,32,512]{2,1,0:T(8,128)} %get-tuple-element.250, s32[]{:T(128)} %get-tuple-element.249, bf16[32,512]{1,0:T(8,128)(2,1)S(1)} %get-tuple-element.279, f32[]{:T(128)} %bitcast.104, f32[512]{0:T(512)S(1)} %bitcast.160, f32[512]{0:T(512)S(1)} %bitcast.162, f32[]{:T(128)} %bitcast.108, ...), kind=kOutput, calls=%fused_computation.1.clone.1 | convolution fusion | flops 31981568 | bytes 163328 | tf_op jit(solution)/shard_map/while/body/eval_jaxpr/dot_general | solution.py:45
  494.7 12.1 %fusion.69 = f32[16,32,512]{2,1,0:T(8,128)} fusion(f32[16,32,512]{2,1,0:T(8,128)} %get-tuple-element.250, s32[]{:T(128)} %get-tuple-element.249, bf16[32,512]{1,0:T(8,128)(2,1)S(1)} %get-tuple-element.279, f32[]{:T(128)} %bitcast.104, f32[512]{0:T(512)S(1)} %bitcast.160, f32[512]{0:T(512)S(1)} %bitcast.162, f32[]{:T(128)} %bitcast.108, ...), kind=kOutput, calls=%fused_computation.1.clone.1 | convolution fusion | flops 31981568 | bytes 163328 | tf_op jit(solution)/shard_map/while/body/eval_jaxpr/dot_general | solution.py:45
  510.0 12.1 %fusion.69 = f32[16,32,512]{2,1,0:T(8,128)} fusion(f32[16,32,512]{2,1,0:T(8,128)} %get-tuple-element.250, s32[]{:T(128)} %get-tuple-element.249, bf16[32,512]{1,0:T(8,128)(2,1)S(1)} %get-tuple-element.279, f32[]{:T(128)} %bitcast.104, f32[512]{0:T(512)S(1)} %bitcast.160, f32[512]{0:T(512)S(1)} %bitcast.162, f32[]{:T(128)} %bitcast.108, ...), kind=kOutput, calls=%fused_computation.1.clone.1 | convolution fusion | flops 31981568 | bytes 163328 | tf_op jit(solution)/shard_map/while/body/eval_jaxpr/dot_general | solution.py:45
  525.4 12.1 %fusion.69 = f32[16,32,512]{2,1,0:T(8,128)} fusion(f32[16,32,512]{2,1,0:T(8,128)} %get-tuple-element.250, s32[]{:T(128)} %get-tuple-element.249, bf16[32,512]{1,0:T(8,128)(2,1)S(1)} %get-tuple-element.279, f32[]{:T(128)} %bitcast.104, f32[512]{0:T(512)S(1)} %bitcast.160, f32[512]{0:T(512)S(1)} %bitcast.162, f32[]{:T(128)} %bitcast.108, ...), kind=kOutput, calls=%fused_computation.1.clone.1 | convolution fusion | flops 31981568 | bytes 163328 | tf_op jit(solution)/shard_map/while/body/eval_jaxpr/dot_general | solution.py:45
  540.7 12.1 %fusion.69 = f32[16,32,512]{2,1,0:T(8,128)} fusion(f32[16,32,512]{2,1,0:T(8,128)} %get-tuple-element.250, s32[]{:T(128)} %get-tuple-element.249, bf16[32,512]{1,0:T(8,128)(2,1)S(1)} %get-tuple-element.279, f32[]{:T(128)} %bitcast.104, f32[512]{0:T(512)S(1)} %bitcast.160, f32[512]{0:T(512)S(1)} %bitcast.162, f32[]{:T(128)} %bitcast.108, ...), kind=kOutput, calls=%fused_computation.1.clone.1 | convolution fusion | flops 31981568 | bytes 163328 | tf_op jit(solution)/shard_map/while/body/eval_jaxpr/dot_general | solution.py:45
  556.1 12.1 %fusion.69 = f32[16,32,512]{2,1,0:T(8,128)} fusion(f32[16,32,512]{2,1,0:T(8,128)} %get-tuple-element.250, s32[]{:T(128)} %get-tuple-element.249, bf16[32,512]{1,0:T(8,128)(2,1)S(1)} %get-tuple-element.279, f32[]{:T(128)} %bitcast.104, f32[512]{0:T(512)S(1)} %bitcast.160, f32[512]{0:T(512)S(1)} %bitcast.162, f32[]{:T(128)} %bitcast.108, ...), kind=kOutput, calls=%fused_computation.1.clone.1 | convolution fusion | flops 31981568 | bytes 163328 | tf_op jit(solution)/shard_map/while/body/eval_jaxpr/dot_general | solution.py:45
  571.4 12.1 %fusion.69 = f32[16,32,512]{2,1,0:T(8,128)} fusion(f32[16,32,512]{2,1,0:T(8,128)} %get-tuple-element.250, s32[]{:T(128)} %get-tuple-element.249, bf16[32,512]{1,0:T(8,128)(2,1)S(1)} %get-tuple-element.279, f32[]{:T(128)} %bitcast.104, f32[512]{0:T(512)S(1)} %bitcast.160, f32[512]{0:T(512)S(1)} %bitcast.162, f32[]{:T(128)} %bitcast.108, ...), kind=kOutput, calls=%fused_computation.1.clone.1 | convolution fusion | flops 31981568 | bytes 163328 | tf_op jit(solution)/shard_map/while/body/eval_jaxpr/dot_general | solution.py:45
  583.5 88.1 %reduce-scatter.2.cloned.1.call-done = f32[1,32,512]{2,1,0:T(8,128)} async-done(((f32[16,32,512]{2,1,0:T(8,128)}), f32[1,32,512]{2,1,0:T(8,128)}) %reduce-scatter.2.cloned.1.call-update) | async-done | bytes 65552 | tf_op jit(solution)/shard_map/reduce_scatter | solution.py:51
  671.6 1.5 bitcast_multiply_fusion
  (86 shorter events, 43.9 us)
Async XLA Ops:
  7.2 169.1 %copy-start = (f32[512,512]{1,0:T(8,128)S(1)}, f32[512,512]{1,0:T(8,128)}, u32[]{:S(2)}) copy-start(f32[512,512]{1,0:T(8,128)} %param.11) | copy-start | bytes 3145732
  7.2 170.7 %copy-start.1 = (f32[512,1024]{1,0:T(8,128)S(1)}, f32[512,1024]{1,0:T(8,128)}, u32[]{:S(2)}) copy-start(f32[512,1024]{1,0:T(8,128)} %param.10) | copy-start | bytes 6291460
  7.2 171.4 %copy-start.3 = (f32[32,512]{1,0:T(8,128)S(1)}, f32[32,512]{1,0:T(8,128)}, u32[]{:S(2)}) copy-start(f32[32,512]{1,0:T(8,128)} %param.9) | copy-start | bytes 196612
  7.2 169.1 %all-reduce.3.cloned.1.call-start = ((), (), s32[]{:S(2)}) async-start(), calls=%async_computation.1 | async-start | bytes 131072 | tf_op jit(solution)/shard_map/psum | solution.py:32
  10.0 325.8 %all-reduce.5.cloned.1.call-start = ((), (), s32[]{:S(2)}) async-start(), calls=%async_computation.2 | async-start | bytes 131072 | tf_op jit(solution)/shard_map/psum | solution.py:35
  177.9 160.1 %copy-start.2 = (f32[14]{0:T(128)S(1)}, f32[14]{0:T(128)}, u32[]{:S(2)}) copy-start(f32[14]{0:T(128)} %param.14) | copy-start | bytes 172
  177.9 160.1 %copy-start.4 = (f32[14,512]{1,0:T(8,128)S(1)}, f32[14,512]{1,0:T(8,128)}, u32[]{:S(2)}) copy-start(f32[14,512]{1,0:T(8,128)} %param.12) | copy-start | bytes 86020
  180.0 491.6 %reduce-scatter.2.cloned.1.call-start = ((), (), s32[]{:S(2)}) async-start(), calls=%async_computation.3 | async-start | bytes 1114112 | tf_op jit(solution)/shard_map/reduce_scatter | solution.py:51
  338.0 333.6 %copy-start.5 = (f32[32]{0:T(128)S(1)}, f32[32]{0:T(128)}, u32[]{:S(2)}) copy-start(f32[32]{0:T(128)} %param.15) | copy-start | bytes 388
Sparse Core Ops, SparseCore 0:
  11.5 164.7 all-reduce.2
  180.1 155.6 all-reduce.4
  583.6 87.9 reduce-scatter.1
where the time goes:
time: 683 us; the launch traced here: 680 us
  waiting for transfers between devices  410 us (60%)
  matrix products  202 us (30%)
  local copies, waits for them, and re-layouts  41.7 us (6%)
  between operations  13.8 us (2%)
  loops' own time  10.8 us (2%)
    dot_general x16, matrix products, single_piece(): jnp.dot(weights_low, kernel_values(train_inputs, chosen, inv_length), pre...  193 us
    psum x1, waiting for transfers between devices, on_device(): rest_one = lax.psum(local_one, 'rows')  166 us
    psum x1, waiting for transfers between devices, on_device(): rest_zero = lax.psum(carried, 'rows')  156 us
    reduce_scatter x1, waiting for transfers between devices, on_device(): lax.psum_scatter(lax.map(single_piece, jnp.arange(1 * lax.axis_size('rows...  88.1 us
    slice x16, local copies, waits for them, and re-layouts, kernel_values(): query_part[dim_index][None, :]  20.7 us
  transfers between devices with their start and end apart: 3, of which 3 were waited for; matrix products, arithmetic and copies ran while one was open for 0% of the time, Pallas kernels for 0%

commit v1 on v0

v1 whole, which is shorter than its diff:
```python
import math

import jax
import jax.numpy as jnp
from jax import lax
from jax.experimental import pallas as pl
from jax.experimental.pallas import tpu as pltpu
from jax.sharding import PartitionSpec as P

F32 = jnp.float32
BF16 = jnp.bfloat16
LOG2E = math.log2(math.e)
FLOOR = 1e-06 * LOG2E * LOG2E


def three_pieces(values):
    high = values.astype(BF16).astype(F32)
    rest = values - high
    middle = rest.astype(BF16).astype(F32)
    low = (rest - middle).astype(BF16).astype(F32)
    return high, middle, low


def extra_rows(rows, count):
    width = rows[0].shape[1]
    index = lax.broadcasted_iota(jnp.int32, (count, width), 0)
    block = jnp.zeros((count, width), F32)
    for place, row in enumerate(rows):
        block = jnp.where(index == place, jnp.broadcast_to(row, (count, width)), block)
    return block


def train_side(points):
    norm = jnp.sum(points * points, axis=0, keepdims=True)
    high, middle, low = (-2.0 * piece for piece in three_pieces(points))
    one = jnp.ones_like(norm)
    extra = extra_rows([one, one, one, *three_pieces(norm)], 32)
    return jnp.concatenate([high, middle, low, high, middle, high, extra], axis=0)


def query_side(points):
    norm = jnp.sum(points * points, axis=0, keepdims=True)
    high, middle, low = three_pieces(points)
    one = jnp.ones_like(norm)
    extra = extra_rows([*three_pieces(norm), one, one, one], 32)
    return jnp.concatenate([high, high, high, middle, middle, low, extra], axis=0)


def kernel_block(train_ref, query_ref, scale_ref, out_ref, left_ref):
    scale = scale_ref[...]

    @pl.when(pl.program_id(0) == 0)
    def _():
        left = train_side((train_ref[...] - 0.5) * scale)
        left_ref[...] = left.T.astype(BF16)

    right = query_side((query_ref[...] - 0.5) * scale).astype(BF16)
    squared = jnp.dot(left_ref[...], right, preferred_element_type=F32)
    squared = jnp.maximum(squared, 0.0) + FLOOR
    out_ref[0] = jnp.exp2(-(squared * lax.rsqrt(squared))).astype(BF16)


def kernel_values(train_inputs, query_points, inv_length, piece):
    params, plans = train_inputs.shape
    queries = query_points.shape[1]
    count = queries // piece
    spare = ((0, 16 - params), (0, 0))
    scale = jnp.pad((inv_length * LOG2E)[:, None], spare)
    return pl.pallas_call(
        kernel_block,
        out_shape=jax.ShapeDtypeStruct((count, plans, piece), BF16),
        grid=(count,),
        in_specs=[
            pl.BlockSpec((16, plans), lambda j: (0, 0)),
            pl.BlockSpec((16, piece), lambda j: (0, j)),
            pl.BlockSpec((16, 1), lambda j: (0, 0)),
        ],
        out_specs=pl.BlockSpec((1, plans, piece), lambda j: (j, 0, 0)),
        scratch_shapes=[pltpu.VMEM((plans, 128), BF16)],
        compiler_params=pltpu.CompilerParams(vmem_limit_bytes=32 * 1024 * 1024),
        cost_estimate=pl.CostEstimate(
            flops=2 * 128 * plans * queries,
            bytes_accessed=2 * plans * queries,
            transcendentals=2 * plans * queries,
        ),
        name="kernel_values",
    )(jnp.pad(train_inputs, spare), jnp.pad(query_points, spare), scale)


def predict_block(weights_ref, kernel_ref, out_ref):
    out_ref[0] = jnp.dot(
        weights_ref[...], kernel_ref[0], preferred_element_type=F32
    ).astype(BF16)


def predictions(weights_low, kernel):
    count, plans, piece = kernel.shape
    rows = weights_low.shape[0]
    return pl.pallas_call(
        predict_block,
        out_shape=jax.ShapeDtypeStruct((count, rows, piece), BF16),
        grid=(count,),
        in_specs=[
            pl.BlockSpec((rows, plans), lambda j: (0, 0)),
            pl.BlockSpec((1, plans, piece), lambda j: (j, 0, 0)),
        ],
        out_specs=pl.BlockSpec((1, rows, piece), lambda j: (j, 0, 0)),
        cost_estimate=pl.CostEstimate(
            flops=2 * rows * plans * piece * count,
            bytes_accessed=2 * plans * piece * count,
            transcendentals=0,
        ),
        name="predictions",
    )(weights_low, kernel)


def product(left, right):
    return jnp.dot(left, right, precision=lax.Precision.HIGH, preferred_element_type=F32)


def on_device(
    coefficients, factor_panel, block_inverse, train_inputs, query_points, inv_length, amplitude
):
    rows, block_len = coefficients.shape
    row_index = lax.axis_index("rows")
    row_count = lax.axis_size("rows")

    partial = jnp.where(row_index >= 2, product(coefficients, factor_panel), 0.0).astype(BF16)
    slots = jnp.concatenate(
        [
            partial[None, :, :block_len],
            partial[None, :, block_len:],
            jnp.zeros((row_count - 2, rows, block_len), BF16),
        ]
    )
    arrived = lax.all_to_all(slots, "rows", 0, 0, tiled=True)
    right_side = coefficients - jnp.sum(arrived.astype(F32), axis=0)
    solved = product(right_side, block_inverse)
    carried = product(solved, factor_panel[:, :block_len])
    carried = lax.ppermute(carried, "rows", [(1, 0)])
    solved = solved - product(carried, block_inverse)
    weights = jnp.where(row_index < 2, solved, coefficients)

    kernel = kernel_values(
        train_inputs, query_points, inv_length, query_points.shape[1] // row_count
    )
    pieces = predictions(weights.astype(BF16), kernel)
    pieces = lax.all_to_all(pieces, "rows", 0, 0, tiled=True)
    predicted_mean = jnp.sum(pieces.astype(F32), axis=0) * amplitude[:, None]
    return (weights, predicted_mean)


def solution(mesh):
    return jax.shard_map(
        on_device,
        mesh=mesh,
        in_specs=(
            P("cols", "rows"),
            P("rows", None),
            P("rows", None),
            P(None, "rows"),
            P(),
            P(),
            P("cols"),
        ),
        out_specs=(P("cols", "rows"), P("cols", "rows")),
        check_vma=False,
    )
```

time: 683 us -> 85.3 us (0.12)
  the two profiles are of different devices: /device:TPU:8 before, /device:TPU:96 now
where the time goes in v1:
time: 85.3 us; the launch traced here: 84.7 us
  blocking collectives  21.4 us (25%)
  Pallas kernels  20.1 us (24%)
  waiting for transfers between devices  18.4 us (22%)
  starting transfers between devices  13.3 us (16%)
  matrix products  5.48 us (6%)
  local copies, waits for them, and re-layouts  3.48 us (4%)
  other arithmetic  1.76 us (2%)
    all_to_all x1, blocking collectives, on_device(): pieces = lax.all_to_all(pieces, 'rows', 0, 0, tiled=True)  21.4 us
    all_to_all x1, waiting for transfers between devices, on_device(): arrived = lax.all_to_all(slots, 'rows', 0, 0, tiled=True)  18.4 us
    all_to_all x1, starting transfers between devices, on_device(): arrived = lax.all_to_all(slots, 'rows', 0, 0, tiled=True)  12 us
    pallas_call x1, Pallas kernels, predictions(): pl.pallas_call(predict_block, out_shape=jax.ShapeDtypeStruct((count, rows...  11.5 us
    pallas_call x1, Pallas kernels, kernel_values(): pl.pallas_call(kernel_block, out_shape=jax.ShapeDtypeStruct((count, plans...  8.54 us
    dot_general x4, matrix products, product(): jnp.dot(left, right, precision=lax.Precision.HIGH, preferred_element_type...  5.48 us
    unnamed x14, local copies, waits for them, and re-layouts  3.25 us
  transfers between devices with their start and end apart: 2, of which 1 were waited for; matrix products, arithmetic and copies ran while one was open for 0% of the time, Pallas kernels for 10%

profile of v1, /device:TPU:96, one launch (start us, length us, event | category | flops | bytes accessed | tf_op | source)
XLA Modules:
  0.0 84.7 jit_solution(3779908593692296635)
XLA Ops:
  0.6 0.0 copy-start
  0.6 0.0 copy-start.6
  0.7 0.0 copy-start.4
  0.7 2.4 %fusion = bf16[32,1024]{1,0:T(8,128)(2,1)S(1)} fusion(f32[32,512]{1,0:T(8,128)} %param.7, f32[512,1024]{1,0:T(8,128)} %param.8, pred[]{:T(512)S(6)} %ge.3), kind=kOutput, calls=%fused_computation.1 | convolution fusion | flops 100728832 | bytes 2228225 | tf_op jit(solution)/shard_map/dot_general | solution.py:118
  3.1 0.0 copy-start.2
  3.2 0.1 pad.17.clone
  3.2 0.9 %maximum_maximum_fusion = bf16[16,32,512]{2,1,0:T(8,128)(2,1)} fusion(bf16[1,32,512]{2,1,0:T(8,128)(2,1)S(1)} %get-tuple-element.3, bf16[1,32,512]{2,1,0:T(8,128)(2,1)S(1)} %get-tuple-element.2, bf16[16]{0:T(256)(128)(2,1)S(1)} %pad.17.clone), kind=kLoop, calls=%fused_computation.8 | loop fusion | flops 524288 | bytes 589856 | tf_op jit(solution)/shard_map/concatenate | solution.py:129
  4.1 12.0 %all-to-all-start = ((bf16[16,32,512]{2,1,0:T(8,128)(2,1)}), bf16[16,32,512]{2,1,0:T(8,128)(2,1)S(1)}, u32[]{:S(2)}, u32[]{:S(2)}) async-start(bf16[16,32,512]{2,1,0:T(8,128)(2,1)} %maximum_maximum_fusion), calls=%async_computation | async-start | bytes 1048576 | tf_op jit(solution)/shard_map/all_to_all | solution.py:136
  16.2 0.1 copy.10
  16.3 0.0 copy-done.4
  16.3 18.4 %all-to-all-done = bf16[16,32,512]{2,1,0:T(8,128)(2,1)S(1)} async-done(((bf16[16,32,512]{2,1,0:T(8,128)(2,1)}), bf16[16,32,512]{2,1,0:T(8,128)(2,1)S(1)}, u32[]{:S(2)}, u32[]{:S(2)}) %all-to-all-start) | async-done | bytes 524320 | tf_op jit(solution)/shard_map/all_to_all | solution.py:136
  34.7 0.1 convert_reduce_fusion.1
  34.8 0.4 fusion.4
  35.2 1.6 %fusion.2 = f32[32,512]{1,0:T(8,128)S(1)} fusion(f32[32,512]{1,0:T(8,128)S(1)} %fusion.4, f32[512,1024]{1,0:T(8,128)} %param.8), kind=kOutput, calls=%fused_computation.5 | convolution fusion | flops 50331648 | bytes 1179648 | tf_op jit(solution)/shard_map/dot_general | solution.py:118
  36.8 1.3 %collective-permute-start = (f32[32,512]{1,0:T(8,128)S(1)}, f32[32,512]{1,0:T(8,128)S(1)}, u32[]{:S(2)}, u32[]{:S(2)}) collective-permute-start(f32[32,512]{1,0:T(8,128)S(1)} %fusion.2), channel_id=1, source_target_pairs={{32,0},{33,1},{34,2},{35,3},{36,4},{37,5},{38,6},{39,7},{40,8},{41... | collective-permute-start | bytes 196616 | tf_op jit(solution)/shard_map/ppermute | solution.py:140
  38.1 8.5 %kernel_values.1.kernel_ref = bf16[16,512,512]{2,1,0:T(8,128)(2,1)S(1)} custom-call(f32[16,512]{1,0:T(8,128)S(1)} %pad.12.train_ref, f32[16,8192]{1,0:T(8,128)S(1)} %pad.13.query_ref, f32[16,1]{1,0:T(8,128)S(1)} %pad.14.scale_ref), custom_call_target="tpu_custom_call" | custom-call | flops 1073741824 | bytes 8388608 | tf_op jit(solution)/shard_map/kernel_values/pallas_call | solution.py:69
  46.7 0.0 copy-start.1
  46.7 3.2 %copy-done.1 = bf16[16,512,512]{2,1,0:T(8,128)(2,1)} copy-done((bf16[16,512,512]{2,1,0:T(8,128)(2,1)}, bf16[16,512,512]{2,1,0:T(8,128)(2,1)S(1)}, u32[]{:S(2)}) %copy-start.1) | copy-done | bytes 8388632
  49.9 0.0 collective-permute-done
  49.9 1.0 %fusion.6 = (bf16[32,512]{1,0:T(8,128)(2,1)}, f32[32,512]{1,0:T(8,128)}) fusion(f32[32,512]{1,0:T(8,128)S(1)} %copy-done.2, f32[32,512]{1,0:T(8,128)S(1)} %fusion.4, f32[32,512]{1,0:T(8,128)S(1)} %collective-permute-done, f32[512,512]{1,0:T(8,128)S(1)} %copy-done, pred[]{:T(512)S(6)} %lt.3), kind=kOutput, calls=%fused_computation.15 | convolution fusion | flops 50380800 | bytes 1343489 | tf_op jit(solution)/shard_map/dot_general | solution.py:118
  51.0 11.5 %predictions.1 = bf16[16,32,512]{2,1,0:T(8,128)(2,1)} custom-call(bf16[32,512]{1,0:T(8,128)(2,1)} %get-tuple-element.4.weights_ref, bf16[16,512,512]{2,1,0:T(8,128)(2,1)} %copy-done.1), custom_call_target="tpu_custom_call" | custom-call | flops 268435456 | bytes 8388608 | tf_op jit(solution)/shard_map/predictions/pallas_call | solution.py:99
  62.5 21.4 %all_to_all.10 = bf16[16,32,512]{2,1,0:T(8,128)(2,1)S(1)} all-to-all(bf16[16,32,512]{2,1,0:T(8,128)(2,1)} %predictions.1), channel_id=1, replica_groups=mesh['rows'=16,'cols'=32] {'rows'}, dimensions={0} | all-to-all | bytes 1048576 | tf_op jit(solution)/shard_map/all_to_all | solution.py:148
  83.9 0.1 convert_reduce_fusion
  84.0 0.7 broadcast_multiply_fusion
  (13 shorter events, 0.1 us)
Async XLA Ops:
  0.6 34.2 %copy-start = (f32[512,512]{1,0:T(8,128)S(1)}, f32[512,512]{1,0:T(8,128)}, u32[]{:S(2)}) copy-start(f32[512,512]{1,0:T(8,128)} %param.9) | copy-start | bytes 3145732
  0.6 15.5 %copy-start.6 = (f32[14]{0:T(128)S(1)}, f32[14]{0:T(128)}, u32[]{:S(2)}) copy-start(f32[14]{0:T(128)} %param.12) | copy-start | bytes 172
  0.7 15.6 %copy-start.4 = (f32[14,512]{1,0:T(8,128)S(1)}, f32[14,512]{1,0:T(8,128)}, u32[]{:S(2)}) copy-start(f32[14,512]{1,0:T(8,128)} %param.10) | copy-start | bytes 86020
  0.7 15.6 %copy-start.3 = (f32[14,8192]{1,0:T(8,128)S(1)}, f32[14,8192]{1,0:T(8,128)}, u32[]{:S(2)}) copy-start(f32[14,8192]{1,0:T(8,128)} %param.11) | copy-start | bytes 1376260
  3.1 31.7 %copy-start.2 = (f32[32,512]{1,0:T(8,128)S(1)}, f32[32,512]{1,0:T(8,128)}, u32[]{:S(2)}) copy-start(f32[32,512]{1,0:T(8,128)} %param.7) | copy-start | bytes 196612
  4.1 30.6 %all-to-all-start = ((bf16[16,32,512]{2,1,0:T(8,128)(2,1)}), bf16[16,32,512]{2,1,0:T(8,128)(2,1)S(1)}, u32[]{:S(2)}, u32[]{:S(2)}) async-start(bf16[16,32,512]{2,1,0:T(8,128)(2,1)} %maximum_maximum_fusion), calls=%async_computation | async-start | bytes 1048576 | tf_op jit(solution)/shard_map/all_to_all | solution.py:136
  36.8 13.1 %collective-permute-start = (f32[32,512]{1,0:T(8,128)S(1)}, f32[32,512]{1,0:T(8,128)S(1)}, u32[]{:S(2)}, u32[]{:S(2)}) collective-permute-start(f32[32,512]{1,0:T(8,128)S(1)} %fusion.2), channel_id=1, source_target_pairs={{32,0},{33,1},{34,2},{35,3},{36,4},{37,5},{38,6},{39,7},{40,8},{41... | collective-permute-start | bytes 196616 | tf_op jit(solution)/shard_map/ppermute | solution.py:140
  46.7 3.2 %copy-start.1 = (bf16[16,512,512]{2,1,0:T(8,128)(2,1)}, bf16[16,512,512]{2,1,0:T(8,128)(2,1)S(1)}, u32[]{:S(2)}) copy-start(bf16[16,512,512]{2,1,0:T(8,128)(2,1)S(1)} %kernel_values.1.kernel_ref) | copy-start | bytes 25165828
  51.0 33.0 %copy-start.5 = (f32[32]{0:T(128)S(1)}, f32[32]{0:T(128)}, u32[]{:S(2)}) copy-start(f32[32]{0:T(128)} %param.13) | copy-start | bytes 388

commit v2 on v0

v2 whole, which is shorter than its diff:
```python
import functools
import math

import jax
import jax.numpy as jnp
from jax import lax
from jax.experimental import pallas as pl
from jax.experimental.pallas import tpu as pltpu
from jax.sharding import PartitionSpec as P

F32 = jnp.float32
BF16 = jnp.bfloat16
LOG2E = math.log2(math.e)
FLOOR = 1e-06 * LOG2E * LOG2E
PADDED = 16
WHOLE = pl.BlockSpec(memory_space=pltpu.VMEM)
SCALARS = pl.BlockSpec(memory_space=pltpu.SMEM)
UNREAD = pl.BlockSpec(memory_space=pl.ANY)
PARAMS = pltpu.CompilerParams(vmem_limit_bytes=16 * 1024 * 1024)

def split(values):
    high = values.astype(BF16)
    return high, (values - high.astype(F32)).astype(BF16)


def dot(left, right):
    return jnp.dot(left, right, preferred_element_type=F32)


def product(left, right_high, right_low):
    rows = left.shape[0]
    left_high, left_low = split(left)
    both = dot(jnp.concatenate([left_high, left_low], axis=0), right_high)
    return both[:rows] + both[rows:] + dot(left_high, right_low)


def three_pieces(values):
    high = values.astype(BF16).astype(F32)
    rest = values - high
    middle = rest.astype(BF16).astype(F32)
    low = (rest - middle).astype(BF16).astype(F32)
    return high, middle, low


def extra_rows(rows, count):
    width = rows[0].shape[1]
    index = lax.broadcasted_iota(jnp.int32, (count, width), 0)
    block = jnp.zeros((count, width), F32)
    for place, row in enumerate(rows):
        block = jnp.where(index == place, jnp.broadcast_to(row, (count, width)), block)
    return block


def train_side(points):
    norm = jnp.sum(points * points, axis=0, keepdims=True)
    high, middle, low = (-2.0 * piece for piece in three_pieces(points))
    one = jnp.ones_like(norm)
    extra = extra_rows([one, one, one, *three_pieces(norm)], 32)
    left = jnp.concatenate([high, middle, low, high, middle, high, extra], axis=0)
    return left.T.astype(BF16)


def query_side(points):
    norm = jnp.sum(points * points, axis=0, keepdims=True)
    high, middle, low = three_pieces(points)
    one = jnp.ones_like(norm)
    extra = extra_rows([*three_pieces(norm), one, one, one], 32)
    right = jnp.concatenate([high, high, high, middle, middle, low, extra], axis=0)
    return right.astype(BF16)


def kernel_values(left, right):
    squared = jnp.maximum(dot(left, right), 0.0) + FLOOR
    return jnp.exp2(-(squared * lax.rsqrt(squared))).astype(BF16)


def scale_column(inv_length_ref):
    index = lax.broadcasted_iota(jnp.int32, (PADDED, 1), 0)
    column = jnp.zeros((PADDED, 1), F32)
    for place in range(inv_length_ref.shape[0]):
        column = jnp.where(index == place, inv_length_ref[place] * LOG2E, column)
    return column


def centred(pad_ref, points):
    pad_ref[...] = jnp.zeros_like(pad_ref)
    pad_ref[: points.shape[0], :] = points - 0.5
    return pad_ref[...]


def residual_kernel(coefficients_ref, factor_ref, train_ref, out_ref, pad_ref):
    row_index = lax.axis_index("rows")
    step = pl.program_id(0)
    width = factor_ref.shape[1]
    parts = out_ref.shape[2] // width

    @pl.when((row_index >= 2) & (step == 0))
    def _():
        out_ref[...] = jnp.zeros_like(out_ref)

    for place in range(2 * parts):
        columns = slice(place % parts * width, (place % parts + 1) * width)

        @pl.when((row_index >= 2) & (step == place))
        def _():
            partial = product(coefficients_ref[...], *split(factor_ref[...]))
            out_ref[place // parts, :, columns] = partial.astype(BF16)

        @pl.when((row_index < 2) & (step == place))
        def _():
            if place < parts:
                both = jnp.concatenate(split(centred(pad_ref, train_ref[...])), axis=0)
                for slot in range(out_ref.shape[0]):
                    out_ref[slot, :, columns] = both


def residuals(coefficients, factor_panel, train_inputs, row_count):
    rows, block_len = coefficients.shape
    width = block_len // 2
    return pl.pallas_call(
        residual_kernel,
        out_shape=jax.ShapeDtypeStruct((row_count, rows, block_len), BF16),
        grid=(4,),
        in_specs=[
            pl.BlockSpec((rows, block_len), lambda j: (0, 0)),
            pl.BlockSpec((block_len, width), lambda j: (0, j)),
            pl.BlockSpec((train_inputs.shape[0], width), lambda j: (0, jnp.minimum(j, 1))),
        ],
        out_specs=pl.BlockSpec((row_count, rows, block_len), lambda j: (0, 0, 0)),
        scratch_shapes=[pltpu.VMEM((PADDED, width), F32)],
        compiler_params=PARAMS,
        name="residuals",
    )(coefficients, factor_panel, train_inputs)


def own_kernel(
    coefficients_ref, train_ref, query_ref, inv_length_ref, inverse_ref, factor_ref,
    out_ref, inverse_high_ref, inverse_low_ref, factor_high_ref, factor_low_ref,
    left_ref, pad_ref, pad_query_ref, stage_ref, sems,
):
    row_index = lax.axis_index("rows")
    count, _, piece = out_ref.shape

    @pl.when(row_index < 2)
    def _():
        width = stage_ref.shape[2]
        copies = [
            pltpu.make_async_copy(inverse_ref, stage_ref.at[0], sems.at[0]),
            pltpu.make_async_copy(factor_ref.at[:, :width], stage_ref.at[1], sems.at[1]),
        ]
        for copy in copies:
            copy.start()
        out_ref[...] = jnp.zeros_like(out_ref)
        for copy in copies:
            copy.wait()
        inverse_high_ref[...], inverse_low_ref[...] = split(stage_ref[0])
        factor_high_ref[...], factor_low_ref[...] = split(stage_ref[1])

    @pl.when(row_index >= 2)
    def _():
        scale = scale_column(inv_length_ref)
        left_ref[...] = train_side(centred(pad_ref, train_ref[...]) * scale)
        low = coefficients_ref[...].astype(BF16)

        def step(place, carry):
            chosen = query_ref[:, pl.ds(pl.multiple_of(place * piece, piece), piece)]
            right = query_side(centred(pad_query_ref, chosen) * scale)
            out_ref[place] = dot(low, kernel_values(left_ref[...], right)).astype(BF16)
            return carry

        lax.fori_loop(0, count, step, 0)


def own_work(coefficients, train_inputs, query_points, inv_length, block_inverse, factor_panel, row_count):
    rows, plans = coefficients.shape
    queries = query_points.shape[1]
    piece = queries // row_count
    square = jax.ShapeDtypeStruct(block_inverse.shape, BF16)
    return pl.pallas_call(
        own_kernel,
        out_shape=(jax.ShapeDtypeStruct((row_count, rows, piece), BF16),) + (square,) * 4,
        in_specs=[WHOLE, WHOLE, WHOLE, SCALARS, UNREAD, UNREAD],
        out_specs=(WHOLE,) * 5,
        scratch_shapes=[
            pltpu.VMEM((plans, 128), BF16),
            pltpu.VMEM((PADDED, plans), F32),
            pltpu.VMEM((PADDED, piece), F32),
            pltpu.VMEM((2, *block_inverse.shape), F32),
            pltpu.SemaphoreType.DMA((2,)),
        ],
        compiler_params=PARAMS,
        cost_estimate=pl.CostEstimate(
            flops=2 * 160 * plans * queries, bytes_accessed=1 << 20, transcendentals=2 * plans * queries
        ),
        name="own_work",
    )(coefficients, train_inputs, query_points, inv_length, block_inverse, factor_panel)


def solve_kernel(
    coefficients_ref, arrived_ref, inverse_high_ref, inverse_low_ref, factor_high_ref, factor_low_ref, out_ref, send_ref
):
    row_index = lax.axis_index("rows")

    @pl.when(row_index < 2)
    def _():
        total = jnp.sum(arrived_ref[2:].astype(F32), axis=0)
        out_ref[...] = product(coefficients_ref[...] - total, inverse_high_ref[...], inverse_low_ref[...])

    @pl.when(row_index == 1)
    def _():
        send_ref[...] = product(out_ref[...], factor_high_ref[...], factor_low_ref[...]).astype(BF16)

    @pl.when(row_index != 1)
    def _():
        send_ref[...] = jnp.zeros_like(send_ref)

    @pl.when(row_index >= 2)
    def _():
        out_ref[...] = coefficients_ref[...]


def solve(coefficients, arrived, squares):
    rows, block_len = coefficients.shape
    return pl.pallas_call(
        solve_kernel,
        out_shape=(
            jax.ShapeDtypeStruct((rows, block_len), F32),
            jax.ShapeDtypeStruct((rows, block_len), BF16),
        ),
        in_specs=[WHOLE] * 6,
        out_specs=(WHOLE, WHOLE),
        compiler_params=PARAMS,
        name="solve",
    )(coefficients, arrived, *squares)


def near_kernel(arrived_ref, query_ref, inv_length_ref, _, kernel_ref, pad_ref):
    scale = scale_column(inv_length_ref)
    right = query_side(centred(pad_ref, query_ref[...]) * scale)
    plans = arrived_ref.shape[2]
    for block in range(2):
        both = arrived_ref[block].astype(F32)
        left = train_side((both[:PADDED] + both[PADDED:]) * scale)
        kernel_ref[block * plans : (block + 1) * plans, :] = kernel_values(left, right)


def near(arrived, own_queries, inv_length, unread):
    plans, queries = arrived.shape[2], own_queries.shape[1]
    return pl.pallas_call(
        near_kernel,
        out_shape=jax.ShapeDtypeStruct((2 * plans, queries), BF16),
        in_specs=[WHOLE, WHOLE, SCALARS, UNREAD],
        out_specs=WHOLE,
        scratch_shapes=[pltpu.VMEM((PADDED, queries), F32)],
        compiler_params=PARAMS,
        cost_estimate=pl.CostEstimate(
            flops=4 * 128 * plans * queries, bytes_accessed=1 << 20, transcendentals=4 * plans * queries
        ),
        name="near",
    )(arrived, own_queries, inv_length, unread)


def correct_kernel(solved_ref, carried_ref, inverse_high_ref, inverse_low_ref, _, __, out_ref, slots_ref, low_ref, sems):
    row_index = lax.axis_index("rows")

    @pl.when(row_index == 0)
    def _():
        carried = carried_ref[...]
        out_ref[...] = solved_ref[...] - (dot(carried, inverse_high_ref[...]) + dot(carried, inverse_low_ref[...]))

    @pl.when(row_index > 0)
    def _():
        out_ref[...] = solved_ref[...]

    @pl.when(row_index < 2)
    def _():
        low_ref[...] = out_ref[...].astype(BF16)
        copies = [
            pltpu.make_async_copy(low_ref, slots_ref.at[slot], sems.at[slot])
            for slot in range(slots_ref.shape[0])
        ]
        for copy in copies:
            copy.start()
        for copy in copies:
            copy.wait()


def correct(solved, carried, inverse_high, inverse_low, slots, unread):
    return pl.pallas_call(
        correct_kernel,
        out_shape=(
            jax.ShapeDtypeStruct(solved.shape, F32),
            jax.ShapeDtypeStruct(slots.shape, slots.dtype),
        ),
        in_specs=[WHOLE] * 4 + [UNREAD] * 2,
        out_specs=(WHOLE, UNREAD),
        input_output_aliases={4: 1},
        scratch_shapes=[
            pltpu.VMEM(solved.shape, BF16),
            pltpu.SemaphoreType.DMA((slots.shape[0],)),
        ],
        compiler_params=PARAMS,
        name="correct",
    )(solved, carried, inverse_high, inverse_low, slots, unread)


def finish_kernel(pieces_ref, kernel_ref, amplitude_ref, mean_ref):
    rows = mean_ref.shape[0]
    plans = kernel_ref.shape[0] // 2
    mean = jnp.sum(pieces_ref[2:].astype(F32), axis=0)
    mean = mean + dot(pieces_ref[0], kernel_ref[:plans, :]) + dot(pieces_ref[1], kernel_ref[plans:, :])
    index = lax.broadcasted_iota(jnp.int32, (rows, 1), 0)
    amplitude = jnp.zeros((rows, 1), F32)
    for row in range(rows):
        amplitude = jnp.where(index == row, amplitude_ref[row], amplitude)
    mean_ref[...] = mean * amplitude


def finish(pieces, kernel, amplitude):
    return pl.pallas_call(
        finish_kernel,
        out_shape=jax.ShapeDtypeStruct(pieces.shape[1:], F32),
        in_specs=[WHOLE, WHOLE, SCALARS],
        out_specs=WHOLE,
        compiler_params=PARAMS,
        name="finish",
    )(pieces, kernel, amplitude)


def on_device(
    coefficients, factor_panel, block_inverse, train_inputs, query_points, inv_length, amplitude
):
    row_index = lax.axis_index("rows")
    row_count = lax.axis_size("rows")
    piece = query_points.shape[1] // row_count

    slots = residuals(coefficients, factor_panel, train_inputs, row_count)
    arrived = lax.all_to_all(slots, "rows", 0, 0, tiled=True)
    slots, *squares = own_work(
        coefficients, train_inputs, query_points, inv_length, block_inverse, factor_panel, row_count
    )
    own_queries = lax.dynamic_slice_in_dim(query_points, row_index * piece, piece, 1)
    solved, carried = solve(coefficients, arrived, squares)
    kernel = near(arrived, own_queries, inv_length, carried)
    carried = lax.ppermute(carried, "rows", [(1, 0)])
    weights, slots = correct(solved, carried, squares[0], squares[1], slots, kernel)
    pieces = lax.all_to_all(slots, "rows", 0, 0, tiled=True)
    return (weights, finish(pieces, kernel, amplitude))


def solution(mesh):
    return jax.shard_map(
        on_device,
        mesh=mesh,
        in_specs=(
            P("cols", "rows"),
            P("rows", None),
            P("rows", None),
            P(None, "rows"),
            P(),
            P(),
            P("cols"),
        ),
        out_specs=(P("cols", "rows"), P("cols", "rows")),
        check_vma=False,
    )
```

time: 683 us -> 71 us (0.10)
  the two profiles are of different devices: /device:TPU:8 before, /device:TPU:64 now
where the time goes in v2:
time: 71 us; the launch traced here: 70.3 us
  blocking collectives  19.3 us (27%)
  waiting for transfers between devices  15.2 us (21%)
  starting transfers between devices  14.1 us (20%)
  local copies, waits for them, and re-layouts  13.6 us (19%)
  Pallas kernels  7.23 us (10%)
  between operations  0.76 us (1%)
    all_to_all x1, blocking collectives, on_device(): pieces = lax.all_to_all(slots, 'rows', 0, 0, tiled=True)  19.3 us
    unnamed x40, local copies, waits for them, and re-layouts  12.8 us
    all_to_all x1, starting transfers between devices, on_device(): arrived = lax.all_to_all(slots, 'rows', 0, 0, tiled=True)  12.7 us
    all_to_all x1, waiting for transfers between devices, on_device(): arrived = lax.all_to_all(slots, 'rows', 0, 0, tiled=True)  11.9 us
    ppermute x1, waiting for transfers between devices, on_device(): carried = lax.ppermute(carried, 'rows', [(1, 0)])  3.28 us
    pallas_call x1, Pallas kernels, correct(): pl.pallas_call(correct_kernel, out_shape=(jax.ShapeDtypeStruct(solved.sha...  1.77 us
    pallas_call x1, Pallas kernels, finish(): pl.pallas_call(finish_kernel, out_shape=jax.ShapeDtypeStruct(pieces.shape...  1.46 us
    ppermute x1, starting transfers between devices, on_device(): carried = lax.ppermute(carried, 'rows', [(1, 0)])  1.43 us
  transfers between devices with their start and end apart: 2, of which 2 were waited for; matrix products, arithmetic and copies ran while one was open for 1% of the time, Pallas kernels for 4%

profile of v2, /device:TPU:64, one launch (start us, length us, event | category | flops | bytes accessed | tf_op | source)
XLA Modules:
  0.0 70.3 jit_solution(7128198919722229420)
XLA Ops:
  0.6 1.6 %copy-done = f32[512,1024]{1,0:T(8,128)S(1)} copy-done((f32[512,1024]{1,0:T(8,128)S(1)}, f32[512,1024]{1,0:T(8,128)}, u32[]{:S(2)}) %copy-start) | copy-done | bytes 2097176
  2.2 0.8 %copy-done.12 = f32[32,512]{1,0:T(8,128)S(1)} copy-done((f32[32,512]{1,0:T(8,128)S(1)}, f32[32,512]{1,0:T(8,128)}, u32[]{:S(2)}) %copy-start.12) | copy-done | bytes 65560
  3.1 0.8 %copy-done.14 = f32[14,512]{1,0:T(8,128)S(1)} copy-done((f32[14,512]{1,0:T(8,128)S(1)}, f32[14,512]{1,0:T(8,128)}, u32[]{:S(2)}) %copy-start.14) | copy-done | bytes 28696
  3.8 1.2 %residuals.1 = bf16[16,32,512]{2,1,0:T(8,128)(2,1)} custom-call(f32[32,512]{1,0:T(8,128)S(1)} %copy-done.12, f32[512,1024]{1,0:T(8,128)S(1)} %copy-done, f32[14,512]{1,0:T(8,128)S(1)} %copy-done.14), custom_call_target="tpu_custom_call" | custom-call | tf_op jit(solution)/shard_map/residuals/pallas_call | solution.py:120
  5.1 12.7 %all-to-all-start = ((bf16[16,32,512]{2,1,0:T(8,128)(2,1)}), bf16[16,32,512]{2,1,0:T(8,128)(2,1)S(1)}, u32[]{:S(2)}, u32[]{:S(2)}) async-start(bf16[16,32,512]{2,1,0:T(8,128)(2,1)} %residuals.1), calls=%async_computation | async-start | bytes 1048576 | tf_op jit(solution)/shard_map/all_to_all | solution.py:338
  17.9 1.0 %copy-done.16 = f32[14,8192]{1,0:T(8,128)S(1)} copy-done((f32[14,8192]{1,0:T(8,128)S(1)}, f32[14,8192]{1,0:T(8,128)}, u32[]{:S(2)}) %copy-start.16) | copy-done | bytes 458776
  18.9 1.2 %copy-done.18 = f32[512,512]{1,0:T(8,128)S(1)} copy-done((f32[512,512]{1,0:T(8,128)S(1)}, f32[512,512]{1,0:T(8,128)}, u32[]{:S(2)}) %copy-start.18) | copy-done | bytes 1048600
  20.1 1.2 %own_work.1 = (bf16[16,32,512]{2,1,0:T(8,128)(2,1)S(1)}, bf16[512,512]{1,0:T(8,128)(2,1)S(1)}, bf16[512,512]{1,0:T(8,128)(2,1)S(1)}, bf16[512,512]{1,0:T(8,128)(2,1)S(1)}, bf16[512,512]{1,0:T(8,128)(2,1)S(1)}) custom-call(f32[32,512]{1,0:T(8,128)S(1)} %copy-done.13, f32[14,512]{1,0:T(8,128)S(1)} %copy-done.15, f32[14,8192]{1,0:T(8,128)S(1)} %copy-done.16, ...), custom_call_target="tpu_custom_call" | custom-call | flops 1342177280 | bytes 1048576 | tf_op jit(solution)/shard_map/own_work/pallas_call | solution.py:179
  21.3 0.8 %copy-done.2 = bf16[512,512]{1,0:T(8,128)(2,1)} copy-done((bf16[512,512]{1,0:T(8,128)(2,1)}, bf16[512,512]{1,0:T(8,128)(2,1)S(1)}, u32[]{:S(2)}) %copy-start.2) | copy-done | bytes 524312
  22.1 0.8 %copy-done.5 = bf16[512,512]{1,0:T(8,128)(2,1)} copy-done((bf16[512,512]{1,0:T(8,128)(2,1)}, bf16[512,512]{1,0:T(8,128)(2,1)S(1)}, u32[]{:S(2)}) %copy-start.5) | copy-done | bytes 524312
  22.9 0.8 %copy-done.8 = bf16[512,512]{1,0:T(8,128)(2,1)} copy-done((bf16[512,512]{1,0:T(8,128)(2,1)}, bf16[512,512]{1,0:T(8,128)(2,1)S(1)}, u32[]{:S(2)}) %copy-start.8) | copy-done | bytes 524312
  23.7 0.8 %copy-done.10 = bf16[512,512]{1,0:T(8,128)(2,1)} copy-done((bf16[512,512]{1,0:T(8,128)(2,1)}, bf16[512,512]{1,0:T(8,128)(2,1)S(1)}, u32[]{:S(2)}) %copy-start.10) | copy-done | bytes 524312
  24.5 11.9 %all-to-all-done.arrived_ref = bf16[16,32,512]{2,1,0:T(8,128)(2,1)S(1)} async-done(((bf16[16,32,512]{2,1,0:T(8,128)(2,1)}), bf16[16,32,512]{2,1,0:T(8,128)(2,1)S(1)}, u32[]{:S(2)}, u32[]{:S(2)}) %all-to-all-start) | async-done | bytes 524320 | tf_op jit(solution)/shard_map/all_to_all | solution.py:338
  36.4 1.0 %copy-done.3 = bf16[512,512]{1,0:T(8,128)(2,1)S(1)} copy-done((bf16[512,512]{1,0:T(8,128)(2,1)S(1)}, bf16[512,512]{1,0:T(8,128)(2,1)}, u32[]{:S(2)}) %copy-start.3) | copy-done | bytes 524312
  37.5 1.0 %copy-done.6 = bf16[512,512]{1,0:T(8,128)(2,1)S(1)} copy-done((bf16[512,512]{1,0:T(8,128)(2,1)S(1)}, bf16[512,512]{1,0:T(8,128)(2,1)}, u32[]{:S(2)}) %copy-start.6) | copy-done | bytes 524312
  38.5 1.0 %copy-done.9 = bf16[512,512]{1,0:T(8,128)(2,1)S(1)} copy-done((bf16[512,512]{1,0:T(8,128)(2,1)S(1)}, bf16[512,512]{1,0:T(8,128)(2,1)}, u32[]{:S(2)}) %copy-start.9) | copy-done | bytes 524312
  39.5 1.0 %copy-done.11 = bf16[512,512]{1,0:T(8,128)(2,1)S(1)} copy-done((bf16[512,512]{1,0:T(8,128)(2,1)S(1)}, bf16[512,512]{1,0:T(8,128)(2,1)}, u32[]{:S(2)}) %copy-start.11) | copy-done | bytes 524312
  40.9 1.4 %collective-permute-start = (bf16[32,512]{1,0:T(8,128)(2,1)S(1)}, bf16[32,512]{1,0:T(8,128)(2,1)S(1)}, u32[]{:S(2)}, u32[]{:S(2)}) collective-permute-start(bf16[32,512]{1,0:T(8,128)(2,1)S(1)} %get-tuple-element.16._), channel_id=1, source_target_pairs={{32,0},{33,1},{34,2},{35,3},{36,4},{37,5},{38,6},{39,7},{40,8},{41... | collective-permute-start | bytes 98312 | tf_op jit(solution)/shard_map/ppermute | solution.py:345
  42.3 0.8 %constant_dynamic-slice_fusion.query_ref = f32[14,512]{1,0:T(8,128)S(1)} fusion(f32[14,8192]{1,0:T(8,128)} %query_ref.1, s32[]{:T(128)S(6)} %select_n.3), kind=kLoop, calls=%fused_computation | loop fusion | bytes 57348 | tf_op jit(solution)/shard_map/dynamic_slice | solution.py:342
  43.1 1.3 %near.1.__.kernel_ref = bf16[1024,512]{1,0:T(8,128)(2,1)S(1)} custom-call(bf16[16,32,512]{2,1,0:T(8,128)(2,1)S(1)} %all-to-all-done.arrived_ref, f32[14,512]{1,0:T(8,128)S(1)} %constant_dynamic-slice_fusion.query_ref, f32[14]{0:T(128)S(1)} %copy-done.19, bf16[32,512]{1,0:T(8,128)(2,1)S(1)} %get-tuple-element.16._), custom_call_target="tpu_custom_call" | custom-call | flops 134217728 | bytes 1048576 | tf_op jit(solution)/shard_map/near/pallas_call | solution.py:249
  44.4 3.3 %collective-permute-done.carried_ref = bf16[32,512]{1,0:T(8,128)(2,1)S(1)} collective-permute-done((bf16[32,512]{1,0:T(8,128)(2,1)S(1)}, bf16[32,512]{1,0:T(8,128)(2,1)S(1)}, u32[]{:S(2)}, u32[]{:S(2)}) %collective-permute-start) | collective-permute-done | bytes 32800 | tf_op jit(solution)/shard_map/ppermute | solution.py:345
  47.7 1.8 %correct.1 = (f32[32,512]{1,0:T(8,128)}, bf16[16,32,512]{2,1,0:T(8,128)(2,1)S(1)}) custom-call(f32[32,512]{1,0:T(8,128)S(1)} %get-tuple-element.15.solved_ref, bf16[32,512]{1,0:T(8,128)(2,1)S(1)} %collective-permute-done.carried_ref, bf16[512,512]{1,0:T(8,128)(2,1)S(1)} %copy-done.4, ...), custom_call_target="tpu_custom_call", output_to_operand_aliasing={{1}: (4, {})} | custom-call | tf_op jit(solution)/shard_map/correct/pallas_call | solution.py:289
  49.5 19.3 %all_to_all.10.pieces_ref = bf16[16,32,512]{2,1,0:T(8,128)(2,1)S(1)} all-to-all(bf16[16,32,512]{2,1,0:T(8,128)(2,1)S(1)} %get-tuple-element.19), channel_id=1, replica_groups=mesh['rows'=16,'cols'=32] {'rows'}, dimensions={0} | all-to-all | bytes 1048576 | tf_op jit(solution)/shard_map/all_to_all | solution.py:347
  68.8 1.5 %finish.1 = f32[32,512]{1,0:T(8,128)} custom-call(bf16[16,32,512]{2,1,0:T(8,128)(2,1)S(1)} %all_to_all.10.pieces_ref, bf16[1024,512]{1,0:T(8,128)(2,1)S(1)} %near.1.__.kernel_ref, f32[32]{0:T(128)S(1)} %copy-done.17), custom_call_target="tpu_custom_call" | custom-call | tf_op jit(solution)/shard_map/finish/pallas_call | solution.py:320
  (28 shorter events, 0.3 us)
Async XLA Ops:
  0.6 1.6 %copy-start = (f32[512,1024]{1,0:T(8,128)S(1)}, f32[512,1024]{1,0:T(8,128)}, u32[]{:S(2)}) copy-start(f32[512,1024]{1,0:T(8,128)} %factor_ref.3) | copy-start | bytes 6291460
  2.2 0.8 %copy-start.12 = (f32[32,512]{1,0:T(8,128)S(1)}, f32[32,512]{1,0:T(8,128)}, u32[]{:S(2)}) copy-start(f32[32,512]{1,0:T(8,128)} %coefficients_ref.5) | copy-start | bytes 196612
  3.1 0.8 %copy-start.14 = (f32[14,512]{1,0:T(8,128)S(1)}, f32[14,512]{1,0:T(8,128)}, u32[]{:S(2)}) copy-start(f32[14,512]{1,0:T(8,128)} %train_ref.3) | copy-start | bytes 86020
  3.8 14.0 %copy-start.1 = (f32[512,1024]{1,0:T(8,128)S(1)}, f32[512,1024]{1,0:T(8,128)}, u32[]{:S(2)}) copy-start(f32[512,1024]{1,0:T(8,128)} %factor_ref.3) | copy-start | bytes 6291460
  3.8 14.0 %copy-start.13 = (f32[32,512]{1,0:T(8,128)S(1)}, f32[32,512]{1,0:T(8,128)}, u32[]{:S(2)}) copy-start(f32[32,512]{1,0:T(8,128)} %coefficients_ref.5) | copy-start | bytes 196612
  3.8 14.0 %copy-start.15 = (f32[14,512]{1,0:T(8,128)S(1)}, f32[14,512]{1,0:T(8,128)}, u32[]{:S(2)}) copy-start(f32[14,512]{1,0:T(8,128)} %train_ref.3) | copy-start | bytes 86020
  3.8 14.0 %copy-start.19 = (f32[14]{0:T(128)S(1)}, f32[14]{0:T(128)}, u32[]{:S(2)}) copy-start(f32[14]{0:T(128)} %inv_length_ref.3) | copy-start | bytes 172
  5.1 31.3 %all-to-all-start = ((bf16[16,32,512]{2,1,0:T(8,128)(2,1)}), bf16[16,32,512]{2,1,0:T(8,128)(2,1)S(1)}, u32[]{:S(2)}, u32[]{:S(2)}) async-start(bf16[16,32,512]{2,1,0:T(8,128)(2,1)} %residuals.1), calls=%async_computation | async-start | bytes 1048576 | tf_op jit(solution)/shard_map/all_to_all | solution.py:338
  17.9 1.0 %copy-start.16 = (f32[14,8192]{1,0:T(8,128)S(1)}, f32[14,8192]{1,0:T(8,128)}, u32[]{:S(2)}) copy-start(f32[14,8192]{1,0:T(8,128)} %query_ref.1) | copy-start | bytes 1376260
  18.9 1.2 %copy-start.18 = (f32[512,512]{1,0:T(8,128)S(1)}, f32[512,512]{1,0:T(8,128)}, u32[]{:S(2)}) copy-start(f32[512,512]{1,0:T(8,128)} %inverse_ref.1) | copy-start | bytes 3145732
  21.3 0.8 %copy-start.2 = (bf16[512,512]{1,0:T(8,128)(2,1)}, bf16[512,512]{1,0:T(8,128)(2,1)S(1)}, u32[]{:S(2)}) copy-start(bf16[512,512]{1,0:T(8,128)(2,1)S(1)} %get-tuple-element.11.inverse_high_ref) | copy-start | bytes 1572868
  22.1 0.8 %copy-start.5 = (bf16[512,512]{1,0:T(8,128)(2,1)}, bf16[512,512]{1,0:T(8,128)(2,1)S(1)}, u32[]{:S(2)}) copy-start(bf16[512,512]{1,0:T(8,128)(2,1)S(1)} %get-tuple-element.12.inverse_low_ref) | copy-start | bytes 1572868
  22.9 0.8 %copy-start.8 = (bf16[512,512]{1,0:T(8,128)(2,1)}, bf16[512,512]{1,0:T(8,128)(2,1)S(1)}, u32[]{:S(2)}) copy-start(bf16[512,512]{1,0:T(8,128)(2,1)S(1)} %get-tuple-element.13.factor_high_ref) | copy-start | bytes 1572868
  23.7 0.8 %copy-start.10 = (bf16[512,512]{1,0:T(8,128)(2,1)}, bf16[512,512]{1,0:T(8,128)(2,1)S(1)}, u32[]{:S(2)}) copy-start(bf16[512,512]{1,0:T(8,128)(2,1)S(1)} %get-tuple-element.14.factor_low_ref) | copy-start | bytes 1572868
  36.4 1.0 %copy-start.3 = (bf16[512,512]{1,0:T(8,128)(2,1)S(1)}, bf16[512,512]{1,0:T(8,128)(2,1)}, u32[]{:S(2)}) copy-start(bf16[512,512]{1,0:T(8,128)(2,1)} %copy-done.2) | copy-start | bytes 1572868
  37.5 1.0 %copy-start.6 = (bf16[512,512]{1,0:T(8,128)(2,1)S(1)}, bf16[512,512]{1,0:T(8,128)(2,1)}, u32[]{:S(2)}) copy-start(bf16[512,512]{1,0:T(8,128)(2,1)} %copy-done.5) | copy-start | bytes 1572868
  38.5 1.0 %copy-start.9 = (bf16[512,512]{1,0:T(8,128)(2,1)S(1)}, bf16[512,512]{1,0:T(8,128)(2,1)}, u32[]{:S(2)}) copy-start(bf16[512,512]{1,0:T(8,128)(2,1)} %copy-done.8) | copy-start | bytes 1572868
  39.5 1.0 %copy-start.11 = (bf16[512,512]{1,0:T(8,128)(2,1)S(1)}, bf16[512,512]{1,0:T(8,128)(2,1)}, u32[]{:S(2)}) copy-start(bf16[512,512]{1,0:T(8,128)(2,1)} %copy-done.10) | copy-start | bytes 1572868
  40.6 7.1 %copy-start.4 = (bf16[512,512]{1,0:T(8,128)(2,1)S(1)}, bf16[512,512]{1,0:T(8,128)(2,1)}, u32[]{:S(2)}) copy-start(bf16[512,512]{1,0:T(8,128)(2,1)} %copy-done.2) | copy-start | bytes 1572868
  40.6 7.1 %copy-start.7 = (bf16[512,512]{1,0:T(8,128)(2,1)S(1)}, bf16[512,512]{1,0:T(8,128)(2,1)}, u32[]{:S(2)}) copy-start(bf16[512,512]{1,0:T(8,128)(2,1)} %copy-done.5) | copy-start | bytes 1572868
  40.9 6.8 %collective-permute-start = (bf16[32,512]{1,0:T(8,128)(2,1)S(1)}, bf16[32,512]{1,0:T(8,128)(2,1)S(1)}, u32[]{:S(2)}, u32[]{:S(2)}) collective-permute-start(bf16[32,512]{1,0:T(8,128)(2,1)S(1)} %get-tuple-element.16._), channel_id=1, source_target_pairs={{32,0},{33,1},{34,2},{35,3},{36,4},{37,5},{38,6},{39,7},{40,8},{41... | collective-permute-start | bytes 98312 | tf_op jit(solution)/shard_map/ppermute | solution.py:345
  44.4 24.4 %copy-start.17 = (f32[32]{0:T(128)S(1)}, f32[32]{0:T(128)}, u32[]{:S(2)}) copy-start(f32[32]{0:T(128)} %amplitude_ref.1) | copy-start | bytes 388

commit v3 on v2

v3 whole, which is shorter than its diff:
```python
import functools
import math

import jax
import jax.numpy as jnp
from jax import lax
from jax.experimental import pallas as pl
from jax.experimental.pallas import tpu as pltpu
from jax.sharding import PartitionSpec as P

F32 = jnp.float32
BF16 = jnp.bfloat16
LOG2E = math.log2(math.e)
FLOOR = 1e-06 * LOG2E * LOG2E
PADDED = 16
WHOLE = pl.BlockSpec(memory_space=pltpu.VMEM)
SCALARS = pl.BlockSpec(memory_space=pltpu.SMEM)
UNREAD = pl.BlockSpec(memory_space=pl.ANY)
PARAMS = pltpu.CompilerParams(vmem_limit_bytes=16 * 1024 * 1024)
ALONE = pltpu.CompilerParams(vmem_limit_bytes=56 * 1024 * 1024)
LINES = range(1, 4)

def split(values):
    high = values.astype(BF16)
    return high, (values - high.astype(F32)).astype(BF16)


def dot(left, right):
    return jnp.dot(left, right, preferred_element_type=F32)


def product(left, right_high, right_low):
    rows = left.shape[0]
    left_high, left_low = split(left)
    both = dot(jnp.concatenate([left_high, left_low], axis=0), right_high)
    return both[:rows] + both[rows:] + dot(left_high, right_low)


def three_pieces(values):
    high = values.astype(BF16).astype(F32)
    rest = values - high
    middle = rest.astype(BF16).astype(F32)
    low = (rest - middle).astype(BF16).astype(F32)
    return high, middle, low


def extra_rows(rows, count):
    width = rows[0].shape[1]
    index = lax.broadcasted_iota(jnp.int32, (count, width), 0)
    block = jnp.zeros((count, width), F32)
    for place, row in enumerate(rows):
        block = jnp.where(index == place, jnp.broadcast_to(row, (count, width)), block)
    return block


def train_side(points):
    norm = jnp.sum(points * points, axis=0, keepdims=True)
    high, middle, low = (-2.0 * piece for piece in three_pieces(points))
    one = jnp.ones_like(norm)
    extra = extra_rows([one, one, one, *three_pieces(norm)], 32)
    left = jnp.concatenate([high, middle, low, high, middle, high, extra], axis=0)
    return left.T.astype(BF16)


def query_side(points):
    norm = jnp.sum(points * points, axis=0, keepdims=True)
    high, middle, low = three_pieces(points)
    one = jnp.ones_like(norm)
    extra = extra_rows([*three_pieces(norm), one, one, one], 32)
    right = jnp.concatenate([high, high, high, middle, middle, low, extra], axis=0)
    return right.astype(BF16)


def kernel_values(left, right):
    squared = jnp.maximum(dot(left, right), 0.0) + FLOOR
    return jnp.exp2(-(squared * lax.rsqrt(squared))).astype(BF16)


def scale_column(inv_length_ref):
    index = lax.broadcasted_iota(jnp.int32, (PADDED, 1), 0)
    column = jnp.zeros((PADDED, 1), F32)
    for place in range(inv_length_ref.shape[0]):
        column = jnp.where(index == place, inv_length_ref[place] * LOG2E, column)
    return column


def centred(pad_ref, points):
    pad_ref[...] = jnp.zeros_like(pad_ref)
    pad_ref[: points.shape[0], :] = points - 0.5
    return pad_ref[...]


def position():
    row_index = lax.axis_index("rows")
    return row_index, row_index // 4, row_index % 4


def residual_kernel(coefficients_ref, factor_ref, out_ref, left_ref, stage_ref, sems):
    row_index, _, _ = position()
    parts, depth, _ = stage_ref.shape

    @pl.when(row_index >= 2)
    def _():
        first = pltpu.make_async_copy(coefficients_ref, left_ref, sems.at[parts])
        first.start()
        copies = [
            pltpu.make_async_copy(
                factor_ref.at[part * depth : (part + 1) * depth, :], stage_ref.at[part], sems.at[part]
            )
            for part in range(parts)
        ]
        for copy in copies:
            copy.start()
        first.wait()
        partial = jnp.zeros(out_ref.shape, F32)
        for part, copy in enumerate(copies):
            left = left_ref[:, part * depth : (part + 1) * depth]
            copy.wait()
            partial = partial + product(left, *split(stage_ref[part]))
        out_ref[...] = partial.astype(BF16)

    @pl.when(row_index < 2)
    def _():
        out_ref[...] = jnp.zeros_like(out_ref)


def residuals(coefficients, factor_panel):
    rows, block_len = coefficients.shape
    parts = 4
    return pl.pallas_call(
        residual_kernel,
        out_shape=jax.ShapeDtypeStruct((rows, 2 * block_len), BF16),
        in_specs=[UNREAD, UNREAD],
        out_specs=WHOLE,
        scratch_shapes=[
            pltpu.VMEM((rows, block_len), F32),
            pltpu.VMEM((parts, block_len // parts, 2 * block_len), F32),
            pltpu.SemaphoreType.DMA((parts + 1,)),
        ],
        compiler_params=ALONE,
        name="residuals",
    )(coefficients, factor_panel)


def combine_kernel(own_ref, first_ref, second_ref, third_ref, sum_ref, *send_refs):
    _, line, place = position()
    block_len = sum_ref.shape[1]

    @pl.when(line == 0)
    def _():
        total = own_ref[...].astype(F32) + first_ref[...].astype(F32)
        total = total + second_ref[...].astype(F32) + third_ref[...].astype(F32)
        for_zero, for_one = total[:, :block_len], total[:, block_len:]
        sum_ref[...] = jnp.where(place == 1, for_one, for_zero)
        for sender, send_ref in zip((0, 2, 3), send_refs):
            send_ref[...] = jnp.where(place == sender, for_one, for_zero).astype(BF16)

    @pl.when(line > 0)
    def _():
        sum_ref[...] = jnp.zeros_like(sum_ref)
        for send_ref in send_refs:
            send_ref[...] = jnp.zeros_like(send_ref)


def combine(own, arrived):
    rows, width = own.shape
    half = (rows, width // 2)
    return pl.pallas_call(
        combine_kernel,
        out_shape=(jax.ShapeDtypeStruct(half, F32),) + (jax.ShapeDtypeStruct(half, BF16),) * 3,
        in_specs=[WHOLE] * 4,
        out_specs=(WHOLE,) * 4,
        compiler_params=PARAMS,
        name="combine",
    )(own, *arrived)


def own_kernel(
    coefficients_ref, train_ref, query_ref, inv_length_ref, _, out_ref, points_ref, left_ref, pad_ref, pad_query_ref
):
    row_index, _, _ = position()
    count, _, piece = out_ref.shape

    @pl.when(row_index < 2)
    def _():
        points_ref[...] = jnp.concatenate(split(centred(pad_ref, train_ref[...])), axis=0)

    @pl.when(row_index >= 2)
    def _():
        scale = scale_column(inv_length_ref)
        left_ref[...] = train_side(centred(pad_ref, train_ref[...]) * scale)
        low = coefficients_ref[...].astype(BF16)

        length = pad_query_ref.shape[1]
        places = length // piece

        def step(part, carry):
            chosen = query_ref[:, pl.ds(pl.multiple_of(part * length, length), length)]
            right = query_side(centred(pad_query_ref, chosen) * scale)
            terms = dot(low, kernel_values(left_ref[...], right)).astype(BF16)
            for place in range(places):
                out_ref[part * places + place] = terms[:, place * piece : (place + 1) * piece]
            return carry

        lax.fori_loop(0, count // places, step, 0)


def own_work(coefficients, train_inputs, query_points, inv_length, row_count, unread):
    rows, plans = coefficients.shape
    queries = query_points.shape[1]
    piece = queries // row_count
    return pl.pallas_call(
        own_kernel,
        out_shape=(
            jax.ShapeDtypeStruct((row_count, rows, piece), BF16),
            jax.ShapeDtypeStruct((2 * PADDED, plans), BF16),
        ),
        in_specs=[WHOLE, WHOLE, WHOLE, SCALARS, UNREAD],
        out_specs=(WHOLE, WHOLE),
        scratch_shapes=[
            pltpu.VMEM((plans, 128), BF16),
            pltpu.VMEM((PADDED, plans), F32),
            pltpu.VMEM((PADDED, 4 * piece), F32),
        ],
        compiler_params=pltpu.CompilerParams(vmem_limit_bytes=24 * 1024 * 1024),
        cost_estimate=pl.CostEstimate(
            flops=2 * 160 * plans * queries, bytes_accessed=1 << 20, transcendentals=2 * plans * queries
        ),
        name="own_work",
    )(coefficients, train_inputs, query_points, inv_length, unread)


def solve_kernel(
    coefficients_ref, sum_ref, first_ref, second_ref, third_ref, inverse_ref, factor_ref,
    points_ref, points_one_ref, points_two_ref, points_three_ref, out_ref, send_ref, held_ref,
):
    row_index, line, _ = position()

    @pl.when(row_index < 2)
    def _():
        total = sum_ref[...] + first_ref[...].astype(F32)
        total = total + second_ref[...].astype(F32) + third_ref[...].astype(F32)
        out_ref[...] = product(coefficients_ref[...] - total, *split(inverse_ref[...]))

    @pl.when(row_index == 1)
    def _():
        send_ref[...] = product(out_ref[...], *split(factor_ref[...])).astype(BF16)

    @pl.when(row_index >= 2)
    def _():
        out_ref[...] = coefficients_ref[...]

    @pl.when(line == 0)
    def _():
        held_ref[...] = points_ref[...]

    for step, arrived_ref in zip(LINES, (points_one_ref, points_two_ref, points_three_ref)):

        @pl.when(line == step)
        def _():
            held_ref[...] = arrived_ref[...]


def solve(coefficients, total, arrived, block_inverse, factor_panel, points):
    rows, block_len = coefficients.shape
    small = pl.BlockSpec((rows, block_len), lambda j: (0, 0))
    square = pl.BlockSpec((block_len, block_len), lambda j: (0, 0))
    pair = pl.BlockSpec(points[0].shape, lambda j: (0, 0))
    return pl.pallas_call(
        solve_kernel,
        out_shape=(
            jax.ShapeDtypeStruct((rows, block_len), F32),
            jax.ShapeDtypeStruct((rows, block_len), BF16),
            jax.ShapeDtypeStruct(points[0].shape, BF16),
        ),
        grid=(1,),
        in_specs=[small] * 5 + [square, square] + [pair] * 4,
        out_specs=(small, small, pair),
        compiler_params=PARAMS,
        name="solve",
    )(coefficients, total, *arrived, block_inverse, factor_panel, *points)


def correct_kernel(solved_ref, carried_ref, inverse_ref, own_ref, points_ref, out_ref, slots_ref, held_ref):
    row_index, _, _ = position()
    held_ref[...] = points_ref[...]

    @pl.when(row_index == 0)
    def _():
        high, low = split(inverse_ref[...])
        carried = carried_ref[...]
        out_ref[...] = solved_ref[...] - (dot(carried, high) + dot(carried, low))

    @pl.when(row_index > 0)
    def _():
        out_ref[...] = solved_ref[...]

    @pl.when(row_index < 2)
    def _():
        low = out_ref[...].astype(BF16)
        for slot in range(slots_ref.shape[0]):
            slots_ref[slot] = low

    @pl.when(row_index >= 2)
    def _():
        slots_ref[...] = own_ref[...]


def correct(solved, carried, block_inverse, own, points):
    return pl.pallas_call(
        correct_kernel,
        out_shape=(
            jax.ShapeDtypeStruct(solved.shape, F32),
            jax.ShapeDtypeStruct(own.shape, own.dtype),
            jax.ShapeDtypeStruct(points.shape, points.dtype),
        ),
        in_specs=[WHOLE] * 5,
        out_specs=(WHOLE,) * 3,
        compiler_params=PARAMS,
        name="correct",
    )(solved, carried, block_inverse, own, points)


def near_kernel(own_ref, first_ref, second_ref, third_ref, query_ref, inv_length_ref, kernel_ref, pad_ref):
    _, _, place = position()
    scale = scale_column(inv_length_ref)
    right = query_side(centred(pad_ref, query_ref[...]) * scale)
    plans = own_ref.shape[1]
    own, first, second, third = (ref[...].astype(F32) for ref in (own_ref, first_ref, second_ref, third_ref))
    zero = jnp.where(place == 0, own, jnp.where(place == 1, first, jnp.where(place == 2, second, third)))
    one = jnp.where(place == 1, own, jnp.where(place == 0, first, jnp.where(place == 3, second, third)))
    for block, both in enumerate((zero, one)):
        left = train_side((both[:PADDED] + both[PADDED:]) * scale)
        kernel_ref[block * plans : (block + 1) * plans, :] = kernel_values(left, right)


def near(own, arrived, own_queries, inv_length):
    plans, queries = own.shape[1], own_queries.shape[1]
    return pl.pallas_call(
        near_kernel,
        out_shape=jax.ShapeDtypeStruct((2 * plans, queries), BF16),
        in_specs=[WHOLE] * 5 + [SCALARS],
        out_specs=WHOLE,
        scratch_shapes=[pltpu.VMEM((PADDED, queries), F32)],
        compiler_params=PARAMS,
        cost_estimate=pl.CostEstimate(
            flops=4 * 128 * plans * queries, bytes_accessed=1 << 20, transcendentals=4 * plans * queries
        ),
        name="near",
    )(own, *arrived, own_queries, inv_length)


def finish_kernel(pieces_ref, kernel_ref, amplitude_ref, mean_ref):
    rows = mean_ref.shape[0]
    plans = kernel_ref.shape[0] // 2
    mean = jnp.sum(pieces_ref[2:].astype(F32), axis=0)
    mean = mean + dot(pieces_ref[0], kernel_ref[:plans, :]) + dot(pieces_ref[1], kernel_ref[plans:, :])
    index = lax.broadcasted_iota(jnp.int32, (rows, 1), 0)
    amplitude = jnp.zeros((rows, 1), F32)
    for row in range(rows):
        amplitude = jnp.where(index == row, amplitude_ref[row], amplitude)
    mean_ref[...] = mean * amplitude


def finish(pieces, kernel, amplitude):
    return pl.pallas_call(
        finish_kernel,
        out_shape=jax.ShapeDtypeStruct(pieces.shape[1:], F32),
        in_specs=[WHOLE, WHOLE, SCALARS],
        out_specs=WHOLE,
        compiler_params=PARAMS,
        name="finish",
    )(pieces, kernel, amplitude)


def on_device(
    coefficients, factor_panel, block_inverse, train_inputs, query_points, inv_length, amplitude
):
    row_index = lax.axis_index("rows")
    row_count = lax.axis_size("rows")
    piece = query_points.shape[1] // row_count
    gathers = (((0, 1), (1, 0)), ((2, 1), (3, 0)), ((3, 1), (2, 0)))
    spreads = (((0, 1), (1, 0)), ((0, 2), (1, 3)), ((0, 3), (1, 2)))

    partial = residuals(coefficients, factor_panel)
    arrived = [lax.ppermute(partial, "rows", [(4 * x + z, z) for z in range(4)]) for x in LINES]
    total, *sends = combine(partial, arrived)
    arrived = [lax.ppermute(send, "rows", pairs) for send, pairs in zip(sends, gathers)]
    own, points = own_work(coefficients, train_inputs, query_points, inv_length, row_count, sends[0])
    points = [points, *(lax.ppermute(points, "rows", [(0, 4 * x), (1, 4 * x + 1)]) for x in LINES)]
    solved, carried, points = solve(coefficients, total, arrived, block_inverse, factor_panel, points)

    carried = lax.ppermute(carried, "rows", [(1, 0)])
    weights, slots, points = correct(solved, carried, block_inverse, own, points)
    pieces = lax.all_to_all(slots, "rows", 0, 0, tiled=True)

    along = [
        lax.ppermute(points, "rows", [(4 * x + a, 4 * x + b) for x in range(4) for a, b in pairs])
        for pairs in spreads
    ]
    own_queries = lax.dynamic_slice_in_dim(query_points, row_index * piece, piece, 1)
    kernel = near(points, along, own_queries, inv_length)
    return (weights, finish(pieces, kernel, amplitude))


def solution(mesh):
    return jax.shard_map(
        on_device,
        mesh=mesh,
        in_specs=(
            P("cols", "rows"),
            P("rows", None),
            P("rows", None),
            P(None, "rows"),
            P(),
            P(),
            P("cols"),
        ),
        out_specs=(P("cols", "rows"), P("cols", "rows")),
        check_vma=False,
    )
```

time: 71 us -> 61.8 us (0.87)
  the two profiles are of different devices: /device:TPU:64 before, /device:TPU:2 now
where the time goes in v3:
time: 61.8 us; the launch traced here: 61.3 us
  starting transfers between devices  34.7 us (56%)
  Pallas kernels  13 us (21%)
  waiting for transfers between devices  11.7 us (19%)
  between operations  0.96 us (2%)
  local copies, waits for them, and re-layouts  0.88 us (1%)
    ppermute x3, starting transfers between devices, on_device(): lax.ppermute(points, 'rows', [(4 * x + a, 4 * x + b) for x in range(4) fo...  11 us
    all_to_all x1, starting transfers between devices, on_device(): pieces = lax.all_to_all(slots, 'rows', 0, 0, tiled=True)  9.69 us
    ppermute x3, starting transfers between devices, on_device(): lax.ppermute(partial, 'rows', [(4 * x + z, z) for z in range(4)])  8.59 us
    pallas_call x1, Pallas kernels, own_work(): pl.pallas_call(own_kernel, out_shape=(jax.ShapeDtypeStruct((row_count, ro...  6.73 us
    ppermute x3, waiting for transfers between devices, on_device(): lax.ppermute(points, 'rows', [(0, 4 * x), (1, 4 * x + 1)])  5.31 us
    ppermute x3, waiting for transfers between devices, on_device(): lax.ppermute(points, 'rows', [(4 * x + a, 4 * x + b) for x in range(4) fo...  4.19 us
    ppermute x3, starting transfers between devices, on_device(): lax.ppermute(points, 'rows', [(0, 4 * x), (1, 4 * x + 1)])  2.62 us
    pallas_call x1, Pallas kernels, residuals(): pl.pallas_call(residual_kernel, out_shape=jax.ShapeDtypeStruct((rows, 2 *...  2.5 us
  transfers between devices with their start and end apart: 14, of which 3 were waited for; matrix products, arithmetic and copies ran while one was open for 0% of the time, Pallas kernels for 13%

profile of v3, /device:TPU:2, one launch (start us, length us, event | category | flops | bytes accessed | tf_op | source)
XLA Modules:
  0.0 61.3 jit_solution(1696427919194597061)
XLA Ops:
  0.7 2.5 %residuals.1.own_ref = bf16[32,1024]{1,0:T(8,128)(2,1)} custom-call(f32[32,512]{1,0:T(8,128)} %coefficients_ref.5, f32[512,1024]{1,0:T(8,128)} %factor_ref.3), custom_call_target="tpu_custom_call" | custom-call | tf_op jit(solution)/shard_map/residuals/pallas_call | solution.py:130
  3.2 0.7 %collective-permute-start.2 = (bf16[32,1024]{1,0:T(8,128)(2,1)}, bf16[32,1024]{1,0:T(8,128)(2,1)S(1)}, u32[]{:S(2)}, u32[]{:S(2)}) collective-permute-start(bf16[32,1024]{1,0:T(8,128)(2,1)} %residuals.1.own_ref), channel_id=1, source_target_pairs={{384,0},{416,32},{448,64},{480,96},{385,1},{417,33},{449,65},{481,... | collective-permute-start | bytes 196616 | tf_op jit(solution)/shard_map/ppermute | solution.py:386
  3.9 0.7 %collective-permute-start.1 = (bf16[32,1024]{1,0:T(8,128)(2,1)}, bf16[32,1024]{1,0:T(8,128)(2,1)S(1)}, u32[]{:S(2)}, u32[]{:S(2)}) collective-permute-start(bf16[32,1024]{1,0:T(8,128)(2,1)} %residuals.1.own_ref), channel_id=1, source_target_pairs={{256,0},{288,32},{320,64},{352,96},{257,1},{289,33},{321,65},{353,... | collective-permute-start | bytes 196616 | tf_op jit(solution)/shard_map/ppermute | solution.py:386
  4.5 7.3 %collective-permute-start = (bf16[32,1024]{1,0:T(8,128)(2,1)}, bf16[32,1024]{1,0:T(8,128)(2,1)S(1)}, u32[]{:S(2)}, u32[]{:S(2)}) collective-permute-start(bf16[32,1024]{1,0:T(8,128)(2,1)} %residuals.1.own_ref), channel_id=1, source_target_pairs={{128,0},{160,32},{192,64},{224,96},{129,1},{161,33},{193,65},{225,... | collective-permute-start | bytes 196616 | tf_op jit(solution)/shard_map/ppermute | solution.py:386
  11.8 2.2 %collective-permute-done.first_ref = bf16[32,1024]{1,0:T(8,128)(2,1)S(1)} collective-permute-done((bf16[32,1024]{1,0:T(8,128)(2,1)}, bf16[32,1024]{1,0:T(8,128)(2,1)S(1)}, u32[]{:S(2)}, u32[]{:S(2)}) %collective-permute-start) | collective-permute-done | bytes 65568 | tf_op jit(solution)/shard_map/ppermute | solution.py:386
  14.0 0.8 %copy-done.3 = bf16[32,1024]{1,0:T(8,128)(2,1)S(1)} copy-done((bf16[32,1024]{1,0:T(8,128)(2,1)S(1)}, bf16[32,1024]{1,0:T(8,128)(2,1)}, u32[]{:S(2)}) %copy-start.3) | copy-done | bytes 65560
  14.9 0.7 %collective-permute-start.4 = (bf16[32,512]{1,0:T(8,128)(2,1)S(1)}, bf16[32,512]{1,0:T(8,128)(2,1)S(1)}, u32[]{:S(2)}, u32[]{:S(2)}) collective-permute-start(bf16[32,512]{1,0:T(8,128)(2,1)S(1)} %get-tuple-element.16), channel_id=1, source_target_pairs={{64,32},{96,0},{65,33},{97,1},{66,34},{98,2},{67,35},{99,3},{68,36... | collective-permute-start | bytes 98312 | tf_op jit(solution)/shard_map/ppermute | solution.py:388
  15.5 0.7 %collective-permute-start.5 = (bf16[32,512]{1,0:T(8,128)(2,1)S(1)}, bf16[32,512]{1,0:T(8,128)(2,1)S(1)}, u32[]{:S(2)}, u32[]{:S(2)}) collective-permute-start(bf16[32,512]{1,0:T(8,128)(2,1)S(1)} %get-tuple-element.17), channel_id=1, source_target_pairs={{96,32},{64,0},{97,33},{65,1},{98,34},{66,2},{99,35},{67,3},{100,3... | collective-permute-start | bytes 98312 | tf_op jit(solution)/shard_map/ppermute | solution.py:388
  16.2 0.8 %collective-permute-start.3 = (bf16[32,512]{1,0:T(8,128)(2,1)S(1)}, bf16[32,512]{1,0:T(8,128)(2,1)S(1)}, u32[]{:S(2)}, u32[]{:S(2)}) collective-permute-start(bf16[32,512]{1,0:T(8,128)(2,1)S(1)} %get-tuple-element.15._), channel_id=1, source_target_pairs={{0,32},{32,0},{1,33},{33,1},{2,34},{34,2},{3,35},{35,3},{4,36},{36... | collective-permute-start | bytes 98312 | tf_op jit(solution)/shard_map/ppermute | solution.py:388
  17.1 6.7 %own_work.1 = (bf16[16,32,512]{2,1,0:T(8,128)(2,1)S(1)}, bf16[32,512]{1,0:T(8,128)(2,1)S(1)}) custom-call(f32[32,512]{1,0:T(8,128)S(1)} %copy-done.2, f32[14,512]{1,0:T(8,128)S(1)} %copy-done.6, f32[14,8192]{1,0:T(8,128)S(1)} %copy-done.4, f32[14]{0:T(128)S(1)} %copy-done.7, bf16[32,512]{1,0:T(8,128)(2,1)S(1)} %get-tuple-element.15._), custom_call_target="tpu_custom_call" | custom-call | flops 1342177280 | bytes 1048576 | tf_op jit(solution)/shard_map/own_work/pallas_call | solution.py:212
  23.8 0.7 %collective-permute-start.8 = (bf16[32,512]{1,0:T(8,128)(2,1)S(1)}, bf16[32,512]{1,0:T(8,128)(2,1)S(1)}, u32[]{:S(2)}, u32[]{:S(2)}) collective-permute-start(bf16[32,512]{1,0:T(8,128)(2,1)S(1)} %get-tuple-element.18.points_ref), channel_id=1, source_target_pairs={{0,384},{32,416},{1,385},{33,417},{2,386},{34,418},{3,387},{35,419... | collective-permute-start | bytes 98312 | tf_op jit(solution)/shard_map/ppermute | solution.py:390
  24.5 0.7 %collective-permute-start.7 = (bf16[32,512]{1,0:T(8,128)(2,1)S(1)}, bf16[32,512]{1,0:T(8,128)(2,1)S(1)}, u32[]{:S(2)}, u32[]{:S(2)}) collective-permute-start(bf16[32,512]{1,0:T(8,128)(2,1)S(1)} %get-tuple-element.18.points_ref), channel_id=1, source_target_pairs={{0,256},{32,288},{1,257},{33,289},{2,258},{34,290},{3,259},{35,291... | collective-permute-start | bytes 98312 | tf_op jit(solution)/shard_map/ppermute | solution.py:390
  25.1 1.3 %collective-permute-start.6 = (bf16[32,512]{1,0:T(8,128)(2,1)S(1)}, bf16[32,512]{1,0:T(8,128)(2,1)S(1)}, u32[]{:S(2)}, u32[]{:S(2)}) collective-permute-start(bf16[32,512]{1,0:T(8,128)(2,1)S(1)} %get-tuple-element.18.points_ref), channel_id=1, source_target_pairs={{0,128},{32,160},{1,129},{33,161},{2,130},{34,162},{3,131},{35,163... | collective-permute-start | bytes 98312 | tf_op jit(solution)/shard_map/ppermute | solution.py:390
  26.5 5.3 %collective-permute-done.6.points_one_ref = bf16[32,512]{1,0:T(8,128)(2,1)S(1)} collective-permute-done((bf16[32,512]{1,0:T(8,128)(2,1)S(1)}, bf16[32,512]{1,0:T(8,128)(2,1)S(1)}, u32[]{:S(2)}, u32[]{:S(2)}) %collective-permute-start.6) | collective-permute-done | bytes 32800 | tf_op jit(solution)/shard_map/ppermute | solution.py:390
  31.8 0.1 solve.1
  31.9 0.7 %collective-permute-start.9 = (bf16[32,512]{1,0:T(8,128)(2,1)S(1)}, bf16[32,512]{1,0:T(8,128)(2,1)S(1)}, u32[]{:S(2)}, u32[]{:S(2)}) collective-permute-start(bf16[32,512]{1,0:T(8,128)(2,1)S(1)} %get-tuple-element.20), channel_id=1, source_target_pairs={{32,0},{33,1},{34,2},{35,3},{36,4},{37,5},{38,6},{39,7},{40,8},{41... | collective-permute-start | bytes 98312 | tf_op jit(solution)/shard_map/ppermute | solution.py:393
  32.6 0.9 %correct.1 = (f32[32,512]{1,0:T(8,128)}, bf16[16,32,512]{2,1,0:T(8,128)(2,1)}, bf16[32,512]{1,0:T(8,128)(2,1)S(1)}) custom-call(f32[32,512]{1,0:T(8,128)S(1)} %get-tuple-element.19.solved_ref, bf16[32,512]{1,0:T(8,128)(2,1)S(1)} %collective-permute-done.9.carried_ref, f32[512,512]{1,0:T(8,128)S(1)} %copy-done.1, ...), custom_call_target="tpu_custom_call" | custom-call | tf_op jit(solution)/shard_map/correct/pallas_call | solution.py:310
  33.5 9.7 %all-to-all-start = ((bf16[16,32,512]{2,1,0:T(8,128)(2,1)}), bf16[16,32,512]{2,1,0:T(8,128)(2,1)S(1)}, u32[]{:S(2)}, u32[]{:S(2)}) async-start(bf16[16,32,512]{2,1,0:T(8,128)(2,1)} %get-tuple-element.24), calls=%async_computation | async-start | bytes 1048576 | tf_op jit(solution)/shard_map/all_to_all | solution.py:395
  43.2 5.5 %collective-permute-start.12 = (bf16[32,512]{1,0:T(8,128)(2,1)S(1)}, bf16[32,512]{1,0:T(8,128)(2,1)S(1)}, u32[]{:S(2)}, u32[]{:S(2)}) collective-permute-start(bf16[32,512]{1,0:T(8,128)(2,1)S(1)} %get-tuple-element.25.own_ref), channel_id=1, source_target_pairs={{0,96},{32,64},{128,224},{160,192},{256,352},{288,320},{384,480},{... | collective-permute-start | bytes 98312 | tf_op jit(solution)/shard_map/ppermute | solution.py:398
  48.7 3.1 %collective-permute-start.11 = (bf16[32,512]{1,0:T(8,128)(2,1)S(1)}, bf16[32,512]{1,0:T(8,128)(2,1)S(1)}, u32[]{:S(2)}, u32[]{:S(2)}) collective-permute-start(bf16[32,512]{1,0:T(8,128)(2,1)S(1)} %get-tuple-element.25.own_ref), channel_id=1, source_target_pairs={{0,64},{32,96},{128,192},{160,224},{256,320},{288,352},{384,448},{... | collective-permute-start | bytes 98312 | tf_op jit(solution)/shard_map/ppermute | solution.py:398
  51.7 2.5 %collective-permute-start.10 = (bf16[32,512]{1,0:T(8,128)(2,1)S(1)}, bf16[32,512]{1,0:T(8,128)(2,1)S(1)}, u32[]{:S(2)}, u32[]{:S(2)}) collective-permute-start(bf16[32,512]{1,0:T(8,128)(2,1)S(1)} %get-tuple-element.25.own_ref), channel_id=1, source_target_pairs={{0,32},{32,0},{128,160},{160,128},{256,288},{288,256},{384,416},{4... | collective-permute-start | bytes 98312 | tf_op jit(solution)/shard_map/ppermute | solution.py:398
  54.3 4.2 %collective-permute-done.10.first_ref = bf16[32,512]{1,0:T(8,128)(2,1)S(1)} collective-permute-done((bf16[32,512]{1,0:T(8,128)(2,1)S(1)}, bf16[32,512]{1,0:T(8,128)(2,1)S(1)}, u32[]{:S(2)}, u32[]{:S(2)}) %collective-permute-start.10) | collective-permute-done | bytes 32800 | tf_op jit(solution)/shard_map/ppermute | solution.py:398
  58.5 1.3 %near.1.kernel_ref = bf16[1024,512]{1,0:T(8,128)(2,1)S(1)} custom-call(bf16[32,512]{1,0:T(8,128)(2,1)S(1)} %get-tuple-element.25.own_ref, bf16[32,512]{1,0:T(8,128)(2,1)S(1)} %collective-permute-done.10.first_ref, bf16[32,512]{1,0:T(8,128)(2,1)S(1)} %collective-permute-done.11.second_ref, bf16[32,512]{1,0:T(8,128)(2,1)S(1)} %collective-permute-done.12.third_ref, ...), custom_call_target="tpu_custom_call" | custom-call | flops 134217728 | bytes 1048576 | tf_op jit(solution)/shard_map/near/pallas_call | solution.py:339
  59.8 1.5 %finish.1 = f32[32,512]{1,0:T(8,128)} custom-call(bf16[16,32,512]{2,1,0:T(8,128)(2,1)S(1)} %all-to-all-done.pieces_ref, bf16[1024,512]{1,0:T(8,128)(2,1)S(1)} %near.1.kernel_ref, f32[32]{0:T(128)S(1)} %copy-done.5), custom_call_target="tpu_custom_call" | custom-call | tf_op jit(solution)/shard_map/finish/pallas_call | solution.py:366
  (28 shorter events, 0.1 us)
Async XLA Ops:
  0.6 16.4 %copy-start.2 = (f32[32,512]{1,0:T(8,128)S(1)}, f32[32,512]{1,0:T(8,128)}, u32[]{:S(2)}) copy-start(f32[32,512]{1,0:T(8,128)} %coefficients_ref.5) | copy-start | bytes 196612
  0.6 16.4 %copy-start.7 = (f32[14]{0:T(128)S(1)}, f32[14]{0:T(128)}, u32[]{:S(2)}) copy-start(f32[14]{0:T(128)} %inv_length_ref.3) | copy-start | bytes 172
  0.7 16.4 %copy-start.4 = (f32[14,8192]{1,0:T(8,128)S(1)}, f32[14,8192]{1,0:T(8,128)}, u32[]{:S(2)}) copy-start(f32[14,8192]{1,0:T(8,128)} %query_ref.1) | copy-start | bytes 1376260
  0.7 16.4 %copy-start.6 = (f32[14,512]{1,0:T(8,128)S(1)}, f32[14,512]{1,0:T(8,128)}, u32[]{:S(2)}) copy-start(f32[14,512]{1,0:T(8,128)} %train_ref.1) | copy-start | bytes 86020
  3.2 8.6 %collective-permute-start.2 = (bf16[32,1024]{1,0:T(8,128)(2,1)}, bf16[32,1024]{1,0:T(8,128)(2,1)S(1)}, u32[]{:S(2)}, u32[]{:S(2)}) collective-permute-start(bf16[32,1024]{1,0:T(8,128)(2,1)} %residuals.1.own_ref), channel_id=1, source_target_pairs={{384,0},{416,32},{448,64},{480,96},{385,1},{417,33},{449,65},{481,... | collective-permute-start | bytes 196616 | tf_op jit(solution)/shard_map/ppermute | solution.py:386
  3.9 8.0 %collective-permute-start.1 = (bf16[32,1024]{1,0:T(8,128)(2,1)}, bf16[32,1024]{1,0:T(8,128)(2,1)S(1)}, u32[]{:S(2)}, u32[]{:S(2)}) collective-permute-start(bf16[32,1024]{1,0:T(8,128)(2,1)} %residuals.1.own_ref), channel_id=1, source_target_pairs={{256,0},{288,32},{320,64},{352,96},{257,1},{289,33},{321,65},{353,... | collective-permute-start | bytes 196616 | tf_op jit(solution)/shard_map/ppermute | solution.py:386
  4.5 9.5 %collective-permute-start = (bf16[32,1024]{1,0:T(8,128)(2,1)}, bf16[32,1024]{1,0:T(8,128)(2,1)S(1)}, u32[]{:S(2)}, u32[]{:S(2)}) collective-permute-start(bf16[32,1024]{1,0:T(8,128)(2,1)} %residuals.1.own_ref), channel_id=1, source_target_pairs={{128,0},{160,32},{192,64},{224,96},{129,1},{161,33},{193,65},{225,... | collective-permute-start | bytes 196616 | tf_op jit(solution)/shard_map/ppermute | solution.py:386
  14.0 0.8 %copy-start.3 = (bf16[32,1024]{1,0:T(8,128)(2,1)S(1)}, bf16[32,1024]{1,0:T(8,128)(2,1)}, u32[]{:S(2)}) copy-start(bf16[32,1024]{1,0:T(8,128)(2,1)} %residuals.1.own_ref) | copy-start | bytes 196612
  14.9 10.3 %collective-permute-start.4 = (bf16[32,512]{1,0:T(8,128)(2,1)S(1)}, bf16[32,512]{1,0:T(8,128)(2,1)S(1)}, u32[]{:S(2)}, u32[]{:S(2)}) collective-permute-start(bf16[32,512]{1,0:T(8,128)(2,1)S(1)} %get-tuple-element.16), channel_id=1, source_target_pairs={{64,32},{96,0},{65,33},{97,1},{66,34},{98,2},{67,35},{99,3},{68,36... | collective-permute-start | bytes 98312 | tf_op jit(solution)/shard_map/ppermute | solution.py:388
  15.5 10.9 %collective-permute-start.5 = (bf16[32,512]{1,0:T(8,128)(2,1)S(1)}, bf16[32,512]{1,0:T(8,128)(2,1)S(1)}, u32[]{:S(2)}, u32[]{:S(2)}) collective-permute-start(bf16[32,512]{1,0:T(8,128)(2,1)S(1)} %get-tuple-element.17), channel_id=1, source_target_pairs={{96,32},{64,0},{97,33},{65,1},{98,34},{66,2},{99,35},{67,3},{100,3... | collective-permute-start | bytes 98312 | tf_op jit(solution)/shard_map/ppermute | solution.py:388
  16.2 15.6 %copy-start = (f32[512,1024]{1,0:T(8,128)S(1)}, f32[512,1024]{1,0:T(8,128)}, u32[]{:S(2)}) copy-start(f32[512,1024]{1,0:T(8,128)} %factor_ref.3) | copy-start | bytes 6291460
  16.2 15.6 %copy-start.1 = (f32[512,512]{1,0:T(8,128)S(1)}, f32[512,512]{1,0:T(8,128)}, u32[]{:S(2)}) copy-start(f32[512,512]{1,0:T(8,128)} %inverse_ref.3) | copy-start | bytes 3145732
  16.2 10.2 %collective-permute-start.3 = (bf16[32,512]{1,0:T(8,128)(2,1)S(1)}, bf16[32,512]{1,0:T(8,128)(2,1)S(1)}, u32[]{:S(2)}, u32[]{:S(2)}) collective-permute-start(bf16[32,512]{1,0:T(8,128)(2,1)S(1)} %get-tuple-element.15._), channel_id=1, source_target_pairs={{0,32},{32,0},{1,33},{33,1},{2,34},{34,2},{3,35},{35,3},{4,36},{36... | collective-permute-start | bytes 98312 | tf_op jit(solution)/shard_map/ppermute | solution.py:388
  23.8 2.7 %collective-permute-start.8 = (bf16[32,512]{1,0:T(8,128)(2,1)S(1)}, bf16[32,512]{1,0:T(8,128)(2,1)S(1)}, u32[]{:S(2)}, u32[]{:S(2)}) collective-permute-start(bf16[32,512]{1,0:T(8,128)(2,1)S(1)} %get-tuple-element.18.points_ref), channel_id=1, source_target_pairs={{0,384},{32,416},{1,385},{33,417},{2,386},{34,418},{3,387},{35,419... | collective-permute-start | bytes 98312 | tf_op jit(solution)/shard_map/ppermute | solution.py:390
  24.5 2.0 %collective-permute-start.7 = (bf16[32,512]{1,0:T(8,128)(2,1)S(1)}, bf16[32,512]{1,0:T(8,128)(2,1)S(1)}, u32[]{:S(2)}, u32[]{:S(2)}) collective-permute-start(bf16[32,512]{1,0:T(8,128)(2,1)S(1)} %get-tuple-element.18.points_ref), channel_id=1, source_target_pairs={{0,256},{32,288},{1,257},{33,289},{2,258},{34,290},{3,259},{35,291... | collective-permute-start | bytes 98312 | tf_op jit(solution)/shard_map/ppermute | solution.py:390
  25.1 6.6 %collective-permute-start.6 = (bf16[32,512]{1,0:T(8,128)(2,1)S(1)}, bf16[32,512]{1,0:T(8,128)(2,1)S(1)}, u32[]{:S(2)}, u32[]{:S(2)}) collective-permute-start(bf16[32,512]{1,0:T(8,128)(2,1)S(1)} %get-tuple-element.18.points_ref), channel_id=1, source_target_pairs={{0,128},{32,160},{1,129},{33,161},{2,130},{34,162},{3,131},{35,163... | collective-permute-start | bytes 98312 | tf_op jit(solution)/shard_map/ppermute | solution.py:390
  31.9 0.7 %collective-permute-start.9 = (bf16[32,512]{1,0:T(8,128)(2,1)S(1)}, bf16[32,512]{1,0:T(8,128)(2,1)S(1)}, u32[]{:S(2)}, u32[]{:S(2)}) collective-permute-start(bf16[32,512]{1,0:T(8,128)(2,1)S(1)} %get-tuple-element.20), channel_id=1, source_target_pairs={{32,0},{33,1},{34,2},{35,3},{36,4},{37,5},{38,6},{39,7},{40,8},{41... | collective-permute-start | bytes 98312 | tf_op jit(solution)/shard_map/ppermute | solution.py:393
  32.6 27.2 %copy-start.5 = (f32[32]{0:T(128)S(1)}, f32[32]{0:T(128)}, u32[]{:S(2)}) copy-start(f32[32]{0:T(128)} %amplitude_ref.1) | copy-start | bytes 388
  33.5 26.3 %all-to-all-start = ((bf16[16,32,512]{2,1,0:T(8,128)(2,1)}), bf16[16,32,512]{2,1,0:T(8,128)(2,1)S(1)}, u32[]{:S(2)}, u32[]{:S(2)}) async-start(bf16[16,32,512]{2,1,0:T(8,128)(2,1)} %get-tuple-element.24), calls=%async_computation | async-start | bytes 1048576 | tf_op jit(solution)/shard_map/all_to_all | solution.py:395
  43.2 11.1 %collective-permute-start.12 = (bf16[32,512]{1,0:T(8,128)(2,1)S(1)}, bf16[32,512]{1,0:T(8,128)(2,1)S(1)}, u32[]{:S(2)}, u32[]{:S(2)}) collective-permute-start(bf16[32,512]{1,0:T(8,128)(2,1)S(1)} %get-tuple-element.25.own_ref), channel_id=1, source_target_pairs={{0,96},{32,64},{128,224},{160,192},{256,352},{288,320},{384,480},{... | collective-permute-start | bytes 98312 | tf_op jit(solution)/shard_map/ppermute | solution.py:398
  48.7 5.6 %collective-permute-start.11 = (bf16[32,512]{1,0:T(8,128)(2,1)S(1)}, bf16[32,512]{1,0:T(8,128)(2,1)S(1)}, u32[]{:S(2)}, u32[]{:S(2)}) collective-permute-start(bf16[32,512]{1,0:T(8,128)(2,1)S(1)} %get-tuple-element.25.own_ref), channel_id=1, source_target_pairs={{0,64},{32,96},{128,192},{160,224},{256,320},{288,352},{384,448},{... | collective-permute-start | bytes 98312 | tf_op jit(solution)/shard_map/ppermute | solution.py:398
  51.7 6.7 %collective-permute-start.10 = (bf16[32,512]{1,0:T(8,128)(2,1)S(1)}, bf16[32,512]{1,0:T(8,128)(2,1)S(1)}, u32[]{:S(2)}, u32[]{:S(2)}) collective-permute-start(bf16[32,512]{1,0:T(8,128)(2,1)S(1)} %get-tuple-element.25.own_ref), channel_id=1, source_target_pairs={{0,32},{32,0},{128,160},{160,128},{256,288},{288,256},{384,416},{4... | collective-permute-start | bytes 98312 | tf_op jit(solution)/shard_map/ppermute | solution.py:398

commit v4 on v3

--- a/solution.py
+++ b/solution.py
@@ -142,14 +142,18 @@
     )(coefficients, factor_panel)
 
 
-def combine_kernel(own_ref, first_ref, second_ref, third_ref, sum_ref, *send_refs):
+def combine_kernel(own_ref, first_ref, second_ref, third_ref, sum_ref, *refs):
+    send_refs, (mine_ref, sem) = refs[:3], refs[3:]
     _, line, place = position()
     block_len = sum_ref.shape[1]
 
     @pl.when(line == 0)
     def _():
-        total = own_ref[...].astype(F32) + first_ref[...].astype(F32)
-        total = total + second_ref[...].astype(F32) + third_ref[...].astype(F32)
+        copy = pltpu.make_async_copy(own_ref, mine_ref, sem.at[0])
+        copy.start()
+        total = first_ref[...].astype(F32) + second_ref[...].astype(F32) + third_ref[...].astype(F32)
+        copy.wait()
+        total = total + mine_ref[...].astype(F32)
         for_zero, for_one = total[:, :block_len], total[:, block_len:]
         sum_ref[...] = jnp.where(place == 1, for_one, for_zero)
         for sender, send_ref in zip((0, 2, 3), send_refs):
@@ -168,8 +172,9 @@
     return pl.pallas_call(
         combine_kernel,
         out_shape=(jax.ShapeDtypeStruct(half, F32),) + (jax.ShapeDtypeStruct(half, BF16),) * 3,
-        in_specs=[WHOLE] * 4,
+        in_specs=[UNREAD] + [WHOLE] * 3,
         out_specs=(WHOLE,) * 4,
+        scratch_shapes=[pltpu.VMEM((rows, width), BF16), pltpu.SemaphoreType.DMA((1,))],
         compiler_params=PARAMS,
         name="combine",
     )(own, *arrived)
@@ -380,7 +385,7 @@
     row_count = lax.axis_size("rows")
     piece = query_points.shape[1] // row_count
     gathers = (((0, 1), (1, 0)), ((2, 1), (3, 0)), ((3, 1), (2, 0)))
-    spreads = (((0, 1), (1, 0)), ((0, 2), (1, 3)), ((0, 3), (1, 2)))
+    spreads = (((0, 3), (1, 2)), ((0, 2), (1, 3)), ((0, 1), (1, 0)))
 
     partial = residuals(coefficients, factor_panel)
     arrived = [lax.ppermute(partial, "rows", [(4 * x + z, z) for z in range(4)]) for x in LINES]
@@ -399,7 +404,7 @@
         for pairs in spreads
     ]
     own_queries = lax.dynamic_slice_in_dim(query_points, row_index * piece, piece, 1)
-    kernel = near(points, along, own_queries, inv_length)
+    kernel = near(points, along[::-1], own_queries, inv_length)
     return (weights, finish(pieces, kernel, amplitude))
 
 

time: 61.8 us -> 61.8 us (level)
  no operation moved by 1% of the time
where the time goes in v4:
time: 61.8 us; the launch traced here: 61.3 us
  starting transfers between devices  34.7 us (56%)
  Pallas kernels  13 us (21%)
  waiting for transfers between devices  11.7 us (19%)
  between operations  0.96 us (2%)
  local copies, waits for them, and re-layouts  0.88 us (1%)
    ppermute x3, starting transfers between devices, on_device(): lax.ppermute(points, 'rows', [(4 * x + a, 4 * x + b) for x in range(4) fo...  11 us
    all_to_all x1, starting transfers between devices, on_device(): pieces = lax.all_to_all(slots, 'rows', 0, 0, tiled=True)  9.69 us
    ppermute x3, starting transfers between devices, on_device(): lax.ppermute(partial, 'rows', [(4 * x + z, z) for z in range(4)])  8.59 us
    pallas_call x1, Pallas kernels, own_work(): pl.pallas_call(own_kernel, out_shape=(jax.ShapeDtypeStruct((row_count, ro...  6.74 us
    ppermute x3, waiting for transfers between devices, on_device(): lax.ppermute(points, 'rows', [(0, 4 * x), (1, 4 * x + 1)])  5.31 us
    ppermute x3, waiting for transfers between devices, on_device(): lax.ppermute(points, 'rows', [(4 * x + a, 4 * x + b) for x in range(4) fo...  4.19 us
    ppermute x3, starting transfers between devices, on_device(): lax.ppermute(points, 'rows', [(0, 4 * x), (1, 4 * x + 1)])  2.62 us
    pallas_call x1, Pallas kernels, residuals(): pl.pallas_call(residual_kernel, out_shape=jax.ShapeDtypeStruct((rows, 2 *...  2.5 us
  transfers between devices with their start and end apart: 14, of which 3 were waited for; matrix products, arithmetic and copies ran while one was open for 0% of the time, Pallas kernels for 13%

profile of v4, /device:TPU:2, one launch (start us, length us, event | category | flops | bytes accessed | tf_op | source)
XLA Modules:
  0.0 61.3 jit_solution(18387806753429190159)
XLA Ops:
  0.7 2.5 %residuals.1.own_ref = bf16[32,1024]{1,0:T(8,128)(2,1)} custom-call(f32[32,512]{1,0:T(8,128)} %coefficients_ref.5, f32[512,1024]{1,0:T(8,128)} %factor_ref.3), custom_call_target="tpu_custom_call" | custom-call | tf_op jit(solution)/shard_map/residuals/pallas_call | solution.py:130
  3.2 0.7 %collective-permute-start.2 = (bf16[32,1024]{1,0:T(8,128)(2,1)}, bf16[32,1024]{1,0:T(8,128)(2,1)S(1)}, u32[]{:S(2)}, u32[]{:S(2)}) collective-permute-start(bf16[32,1024]{1,0:T(8,128)(2,1)} %residuals.1.own_ref), channel_id=1, source_target_pairs={{384,0},{416,32},{448,64},{480,96},{385,1},{417,33},{449,65},{481,... | collective-permute-start | bytes 196616 | tf_op jit(solution)/shard_map/ppermute | solution.py:391
  3.9 0.7 %collective-permute-start.1 = (bf16[32,1024]{1,0:T(8,128)(2,1)}, bf16[32,1024]{1,0:T(8,128)(2,1)S(1)}, u32[]{:S(2)}, u32[]{:S(2)}) collective-permute-start(bf16[32,1024]{1,0:T(8,128)(2,1)} %residuals.1.own_ref), channel_id=1, source_target_pairs={{256,0},{288,32},{320,64},{352,96},{257,1},{289,33},{321,65},{353,... | collective-permute-start | bytes 196616 | tf_op jit(solution)/shard_map/ppermute | solution.py:391
  4.5 7.3 %collective-permute-start = (bf16[32,1024]{1,0:T(8,128)(2,1)}, bf16[32,1024]{1,0:T(8,128)(2,1)S(1)}, u32[]{:S(2)}, u32[]{:S(2)}) collective-permute-start(bf16[32,1024]{1,0:T(8,128)(2,1)} %residuals.1.own_ref), channel_id=1, source_target_pairs={{128,0},{160,32},{192,64},{224,96},{129,1},{161,33},{193,65},{225,... | collective-permute-start | bytes 196616 | tf_op jit(solution)/shard_map/ppermute | solution.py:391
  11.8 2.2 %collective-permute-done.first_ref = bf16[32,1024]{1,0:T(8,128)(2,1)S(1)} collective-permute-done((bf16[32,1024]{1,0:T(8,128)(2,1)}, bf16[32,1024]{1,0:T(8,128)(2,1)S(1)}, u32[]{:S(2)}, u32[]{:S(2)}) %collective-permute-start) | collective-permute-done | bytes 65568 | tf_op jit(solution)/shard_map/ppermute | solution.py:391
  14.0 0.8 %copy-done.3 = bf16[32,1024]{1,0:T(8,128)(2,1)S(1)} copy-done((bf16[32,1024]{1,0:T(8,128)(2,1)S(1)}, bf16[32,1024]{1,0:T(8,128)(2,1)}, u32[]{:S(2)}) %copy-start.3) | copy-done | bytes 65560
  14.9 0.7 %collective-permute-start.4 = (bf16[32,512]{1,0:T(8,128)(2,1)S(1)}, bf16[32,512]{1,0:T(8,128)(2,1)S(1)}, u32[]{:S(2)}, u32[]{:S(2)}) collective-permute-start(bf16[32,512]{1,0:T(8,128)(2,1)S(1)} %get-tuple-element.16), channel_id=1, source_target_pairs={{64,32},{96,0},{65,33},{97,1},{66,34},{98,2},{67,35},{99,3},{68,36... | collective-permute-start | bytes 98312 | tf_op jit(solution)/shard_map/ppermute | solution.py:393
  15.5 0.7 %collective-permute-start.5 = (bf16[32,512]{1,0:T(8,128)(2,1)S(1)}, bf16[32,512]{1,0:T(8,128)(2,1)S(1)}, u32[]{:S(2)}, u32[]{:S(2)}) collective-permute-start(bf16[32,512]{1,0:T(8,128)(2,1)S(1)} %get-tuple-element.17), channel_id=1, source_target_pairs={{96,32},{64,0},{97,33},{65,1},{98,34},{66,2},{99,35},{67,3},{100,3... | collective-permute-start | bytes 98312 | tf_op jit(solution)/shard_map/ppermute | solution.py:393
  16.2 0.8 %collective-permute-start.3 = (bf16[32,512]{1,0:T(8,128)(2,1)S(1)}, bf16[32,512]{1,0:T(8,128)(2,1)S(1)}, u32[]{:S(2)}, u32[]{:S(2)}) collective-permute-start(bf16[32,512]{1,0:T(8,128)(2,1)S(1)} %get-tuple-element.15._), channel_id=1, source_target_pairs={{0,32},{32,0},{1,33},{33,1},{2,34},{34,2},{3,35},{35,3},{4,36},{36... | collective-permute-start | bytes 98312 | tf_op jit(solution)/shard_map/ppermute | solution.py:393
  17.1 6.7 %own_work.1 = (bf16[16,32,512]{2,1,0:T(8,128)(2,1)S(1)}, bf16[32,512]{1,0:T(8,128)(2,1)S(1)}) custom-call(f32[32,512]{1,0:T(8,128)S(1)} %copy-done.2, f32[14,512]{1,0:T(8,128)S(1)} %copy-done.6, f32[14,8192]{1,0:T(8,128)S(1)} %copy-done.4, f32[14]{0:T(128)S(1)} %copy-done.7, bf16[32,512]{1,0:T(8,128)(2,1)S(1)} %get-tuple-element.15._), custom_call_target="tpu_custom_call" | custom-call | flops 1342177280 | bytes 1048576 | tf_op jit(solution)/shard_map/own_work/pallas_call | solution.py:217
  23.8 0.7 %collective-permute-start.8 = (bf16[32,512]{1,0:T(8,128)(2,1)S(1)}, bf16[32,512]{1,0:T(8,128)(2,1)S(1)}, u32[]{:S(2)}, u32[]{:S(2)}) collective-permute-start(bf16[32,512]{1,0:T(8,128)(2,1)S(1)} %get-tuple-element.18.points_ref), channel_id=1, source_target_pairs={{0,384},{32,416},{1,385},{33,417},{2,386},{34,418},{3,387},{35,419... | collective-permute-start | bytes 98312 | tf_op jit(solution)/shard_map/ppermute | solution.py:395
  24.5 0.7 %collective-permute-start.7 = (bf16[32,512]{1,0:T(8,128)(2,1)S(1)}, bf16[32,512]{1,0:T(8,128)(2,1)S(1)}, u32[]{:S(2)}, u32[]{:S(2)}) collective-permute-start(bf16[32,512]{1,0:T(8,128)(2,1)S(1)} %get-tuple-element.18.points_ref), channel_id=1, source_target_pairs={{0,256},{32,288},{1,257},{33,289},{2,258},{34,290},{3,259},{35,291... | collective-permute-start | bytes 98312 | tf_op jit(solution)/shard_map/ppermute | solution.py:395
  25.2 1.3 %collective-permute-start.6 = (bf16[32,512]{1,0:T(8,128)(2,1)S(1)}, bf16[32,512]{1,0:T(8,128)(2,1)S(1)}, u32[]{:S(2)}, u32[]{:S(2)}) collective-permute-start(bf16[32,512]{1,0:T(8,128)(2,1)S(1)} %get-tuple-element.18.points_ref), channel_id=1, source_target_pairs={{0,128},{32,160},{1,129},{33,161},{2,130},{34,162},{3,131},{35,163... | collective-permute-start | bytes 98312 | tf_op jit(solution)/shard_map/ppermute | solution.py:395
  26.5 5.3 %collective-permute-done.6.points_one_ref = bf16[32,512]{1,0:T(8,128)(2,1)S(1)} collective-permute-done((bf16[32,512]{1,0:T(8,128)(2,1)S(1)}, bf16[32,512]{1,0:T(8,128)(2,1)S(1)}, u32[]{:S(2)}, u32[]{:S(2)}) %collective-permute-start.6) | collective-permute-done | bytes 32800 | tf_op jit(solution)/shard_map/ppermute | solution.py:395
  31.8 0.1 solve.1
  31.9 0.7 %collective-permute-start.9 = (bf16[32,512]{1,0:T(8,128)(2,1)S(1)}, bf16[32,512]{1,0:T(8,128)(2,1)S(1)}, u32[]{:S(2)}, u32[]{:S(2)}) collective-permute-start(bf16[32,512]{1,0:T(8,128)(2,1)S(1)} %get-tuple-element.20), channel_id=1, source_target_pairs={{32,0},{33,1},{34,2},{35,3},{36,4},{37,5},{38,6},{39,7},{40,8},{41... | collective-permute-start | bytes 98312 | tf_op jit(solution)/shard_map/ppermute | solution.py:398
  32.6 0.9 %correct.1 = (f32[32,512]{1,0:T(8,128)}, bf16[16,32,512]{2,1,0:T(8,128)(2,1)}, bf16[32,512]{1,0:T(8,128)(2,1)S(1)}) custom-call(f32[32,512]{1,0:T(8,128)S(1)} %get-tuple-element.19.solved_ref, bf16[32,512]{1,0:T(8,128)(2,1)S(1)} %collective-permute-done.9.carried_ref, f32[512,512]{1,0:T(8,128)S(1)} %copy-done.1, ...), custom_call_target="tpu_custom_call" | custom-call | tf_op jit(solution)/shard_map/correct/pallas_call | solution.py:315
  33.5 9.7 %all-to-all-start = ((bf16[16,32,512]{2,1,0:T(8,128)(2,1)}), bf16[16,32,512]{2,1,0:T(8,128)(2,1)S(1)}, u32[]{:S(2)}, u32[]{:S(2)}) async-start(bf16[16,32,512]{2,1,0:T(8,128)(2,1)} %get-tuple-element.24), calls=%async_computation | async-start | bytes 1048576 | tf_op jit(solution)/shard_map/all_to_all | solution.py:400
  43.2 5.5 %collective-permute-start.12 = (bf16[32,512]{1,0:T(8,128)(2,1)S(1)}, bf16[32,512]{1,0:T(8,128)(2,1)S(1)}, u32[]{:S(2)}, u32[]{:S(2)}) collective-permute-start(bf16[32,512]{1,0:T(8,128)(2,1)S(1)} %get-tuple-element.25.own_ref), channel_id=1, source_target_pairs={{0,96},{32,64},{128,224},{160,192},{256,352},{288,320},{384,480},{... | collective-permute-start | bytes 98312 | tf_op jit(solution)/shard_map/ppermute | solution.py:403
  48.7 3.1 %collective-permute-start.11 = (bf16[32,512]{1,0:T(8,128)(2,1)S(1)}, bf16[32,512]{1,0:T(8,128)(2,1)S(1)}, u32[]{:S(2)}, u32[]{:S(2)}) collective-permute-start(bf16[32,512]{1,0:T(8,128)(2,1)S(1)} %get-tuple-element.25.own_ref), channel_id=1, source_target_pairs={{0,64},{32,96},{128,192},{160,224},{256,320},{288,352},{384,448},{... | collective-permute-start | bytes 98312 | tf_op jit(solution)/shard_map/ppermute | solution.py:403
  51.8 2.5 %collective-permute-start.10 = (bf16[32,512]{1,0:T(8,128)(2,1)S(1)}, bf16[32,512]{1,0:T(8,128)(2,1)S(1)}, u32[]{:S(2)}, u32[]{:S(2)}) collective-permute-start(bf16[32,512]{1,0:T(8,128)(2,1)S(1)} %get-tuple-element.25.own_ref), channel_id=1, source_target_pairs={{0,32},{32,0},{128,160},{160,128},{256,288},{288,256},{384,416},{4... | collective-permute-start | bytes 98312 | tf_op jit(solution)/shard_map/ppermute | solution.py:403
  54.3 4.2 %collective-permute-done.10.first_ref = bf16[32,512]{1,0:T(8,128)(2,1)S(1)} collective-permute-done((bf16[32,512]{1,0:T(8,128)(2,1)S(1)}, bf16[32,512]{1,0:T(8,128)(2,1)S(1)}, u32[]{:S(2)}, u32[]{:S(2)}) %collective-permute-start.10) | collective-permute-done | bytes 32800 | tf_op jit(solution)/shard_map/ppermute | solution.py:403
  58.5 1.3 %near.1.kernel_ref = bf16[1024,512]{1,0:T(8,128)(2,1)S(1)} custom-call(bf16[32,512]{1,0:T(8,128)(2,1)S(1)} %get-tuple-element.25.own_ref, bf16[32,512]{1,0:T(8,128)(2,1)S(1)} %collective-permute-done.10.first_ref, bf16[32,512]{1,0:T(8,128)(2,1)S(1)} %collective-permute-done.11.second_ref, bf16[32,512]{1,0:T(8,128)(2,1)S(1)} %collective-permute-done.12.third_ref, ...), custom_call_target="tpu_custom_call" | custom-call | flops 134217728 | bytes 1048576 | tf_op jit(solution)/shard_map/near/pallas_call | solution.py:344
  59.8 1.5 %finish.1 = f32[32,512]{1,0:T(8,128)} custom-call(bf16[16,32,512]{2,1,0:T(8,128)(2,1)S(1)} %all-to-all-done.pieces_ref, bf16[1024,512]{1,0:T(8,128)(2,1)S(1)} %near.1.kernel_ref, f32[32]{0:T(128)S(1)} %copy-done.5), custom_call_target="tpu_custom_call" | custom-call | tf_op jit(solution)/shard_map/finish/pallas_call | solution.py:371
  (28 shorter events, 0.1 us)
Async XLA Ops:
  0.6 16.4 %copy-start.2 = (f32[32,512]{1,0:T(8,128)S(1)}, f32[32,512]{1,0:T(8,128)}, u32[]{:S(2)}) copy-start(f32[32,512]{1,0:T(8,128)} %coefficients_ref.5) | copy-start | bytes 196612
  0.6 16.4 %copy-start.7 = (f32[14]{0:T(128)S(1)}, f32[14]{0:T(128)}, u32[]{:S(2)}) copy-start(f32[14]{0:T(128)} %inv_length_ref.3) | copy-start | bytes 172
  0.7 16.4 %copy-start.4 = (f32[14,8192]{1,0:T(8,128)S(1)}, f32[14,8192]{1,0:T(8,128)}, u32[]{:S(2)}) copy-start(f32[14,8192]{1,0:T(8,128)} %query_ref.1) | copy-start | bytes 1376260
  0.7 16.4 %copy-start.6 = (f32[14,512]{1,0:T(8,128)S(1)}, f32[14,512]{1,0:T(8,128)}, u32[]{:S(2)}) copy-start(f32[14,512]{1,0:T(8,128)} %train_ref.1) | copy-start | bytes 86020
  3.2 8.6 %collective-permute-start.2 = (bf16[32,1024]{1,0:T(8,128)(2,1)}, bf16[32,1024]{1,0:T(8,128)(2,1)S(1)}, u32[]{:S(2)}, u32[]{:S(2)}) collective-permute-start(bf16[32,1024]{1,0:T(8,128)(2,1)} %residuals.1.own_ref), channel_id=1, source_target_pairs={{384,0},{416,32},{448,64},{480,96},{385,1},{417,33},{449,65},{481,... | collective-permute-start | bytes 196616 | tf_op jit(solution)/shard_map/ppermute | solution.py:391
  3.9 8.0 %collective-permute-start.1 = (bf16[32,1024]{1,0:T(8,128)(2,1)}, bf16[32,1024]{1,0:T(8,128)(2,1)S(1)}, u32[]{:S(2)}, u32[]{:S(2)}) collective-permute-start(bf16[32,1024]{1,0:T(8,128)(2,1)} %residuals.1.own_ref), channel_id=1, source_target_pairs={{256,0},{288,32},{320,64},{352,96},{257,1},{289,33},{321,65},{353,... | collective-permute-start | bytes 196616 | tf_op jit(solution)/shard_map/ppermute | solution.py:391
  4.5 9.5 %collective-permute-start = (bf16[32,1024]{1,0:T(8,128)(2,1)}, bf16[32,1024]{1,0:T(8,128)(2,1)S(1)}, u32[]{:S(2)}, u32[]{:S(2)}) collective-permute-start(bf16[32,1024]{1,0:T(8,128)(2,1)} %residuals.1.own_ref), channel_id=1, source_target_pairs={{128,0},{160,32},{192,64},{224,96},{129,1},{161,33},{193,65},{225,... | collective-permute-start | bytes 196616 | tf_op jit(solution)/shard_map/ppermute | solution.py:391
  14.0 0.8 %copy-start.3 = (bf16[32,1024]{1,0:T(8,128)(2,1)S(1)}, bf16[32,1024]{1,0:T(8,128)(2,1)}, u32[]{:S(2)}) copy-start(bf16[32,1024]{1,0:T(8,128)(2,1)} %residuals.1.own_ref) | copy-start | bytes 196612
  14.9 10.3 %collective-permute-start.4 = (bf16[32,512]{1,0:T(8,128)(2,1)S(1)}, bf16[32,512]{1,0:T(8,128)(2,1)S(1)}, u32[]{:S(2)}, u32[]{:S(2)}) collective-permute-start(bf16[32,512]{1,0:T(8,128)(2,1)S(1)} %get-tuple-element.16), channel_id=1, source_target_pairs={{64,32},{96,0},{65,33},{97,1},{66,34},{98,2},{67,35},{99,3},{68,36... | collective-permute-start | bytes 98312 | tf_op jit(solution)/shard_map/ppermute | solution.py:393
  15.5 10.9 %collective-permute-start.5 = (bf16[32,512]{1,0:T(8,128)(2,1)S(1)}, bf16[32,512]{1,0:T(8,128)(2,1)S(1)}, u32[]{:S(2)}, u32[]{:S(2)}) collective-permute-start(bf16[32,512]{1,0:T(8,128)(2,1)S(1)} %get-tuple-element.17), channel_id=1, source_target_pairs={{96,32},{64,0},{97,33},{65,1},{98,34},{66,2},{99,35},{67,3},{100,3... | collective-permute-start | bytes 98312 | tf_op jit(solution)/shard_map/ppermute | solution.py:393
  16.2 15.6 %copy-start = (f32[512,1024]{1,0:T(8,128)S(1)}, f32[512,1024]{1,0:T(8,128)}, u32[]{:S(2)}) copy-start(f32[512,1024]{1,0:T(8,128)} %factor_ref.3) | copy-start | bytes 6291460
  16.2 15.6 %copy-start.1 = (f32[512,512]{1,0:T(8,128)S(1)}, f32[512,512]{1,0:T(8,128)}, u32[]{:S(2)}) copy-start(f32[512,512]{1,0:T(8,128)} %inverse_ref.3) | copy-start | bytes 3145732
  16.2 10.2 %collective-permute-start.3 = (bf16[32,512]{1,0:T(8,128)(2,1)S(1)}, bf16[32,512]{1,0:T(8,128)(2,1)S(1)}, u32[]{:S(2)}, u32[]{:S(2)}) collective-permute-start(bf16[32,512]{1,0:T(8,128)(2,1)S(1)} %get-tuple-element.15._), channel_id=1, source_target_pairs={{0,32},{32,0},{1,33},{33,1},{2,34},{34,2},{3,35},{35,3},{4,36},{36... | collective-permute-start | bytes 98312 | tf_op jit(solution)/shard_map/ppermute | solution.py:393
  23.8 2.7 %collective-permute-start.8 = (bf16[32,512]{1,0:T(8,128)(2,1)S(1)}, bf16[32,512]{1,0:T(8,128)(2,1)S(1)}, u32[]{:S(2)}, u32[]{:S(2)}) collective-permute-start(bf16[32,512]{1,0:T(8,128)(2,1)S(1)} %get-tuple-element.18.points_ref), channel_id=1, source_target_pairs={{0,384},{32,416},{1,385},{33,417},{2,386},{34,418},{3,387},{35,419... | collective-permute-start | bytes 98312 | tf_op jit(solution)/shard_map/ppermute | solution.py:395
  24.5 2.0 %collective-permute-start.7 = (bf16[32,512]{1,0:T(8,128)(2,1)S(1)}, bf16[32,512]{1,0:T(8,128)(2,1)S(1)}, u32[]{:S(2)}, u32[]{:S(2)}) collective-permute-start(bf16[32,512]{1,0:T(8,128)(2,1)S(1)} %get-tuple-element.18.points_ref), channel_id=1, source_target_pairs={{0,256},{32,288},{1,257},{33,289},{2,258},{34,290},{3,259},{35,291... | collective-permute-start | bytes 98312 | tf_op jit(solution)/shard_map/ppermute | solution.py:395
  25.2 6.6 %collective-permute-start.6 = (bf16[32,512]{1,0:T(8,128)(2,1)S(1)}, bf16[32,512]{1,0:T(8,128)(2,1)S(1)}, u32[]{:S(2)}, u32[]{:S(2)}) collective-permute-start(bf16[32,512]{1,0:T(8,128)(2,1)S(1)} %get-tuple-element.18.points_ref), channel_id=1, source_target_pairs={{0,128},{32,160},{1,129},{33,161},{2,130},{34,162},{3,131},{35,163... | collective-permute-start | bytes 98312 | tf_op jit(solution)/shard_map/ppermute | solution.py:395
  31.9 0.7 %collective-permute-start.9 = (bf16[32,512]{1,0:T(8,128)(2,1)S(1)}, bf16[32,512]{1,0:T(8,128)(2,1)S(1)}, u32[]{:S(2)}, u32[]{:S(2)}) collective-permute-start(bf16[32,512]{1,0:T(8,128)(2,1)S(1)} %get-tuple-element.20), channel_id=1, source_target_pairs={{32,0},{33,1},{34,2},{35,3},{36,4},{37,5},{38,6},{39,7},{40,8},{41... | collective-permute-start | bytes 98312 | tf_op jit(solution)/shard_map/ppermute | solution.py:398
  32.6 27.2 %copy-start.5 = (f32[32]{0:T(128)S(1)}, f32[32]{0:T(128)}, u32[]{:S(2)}) copy-start(f32[32]{0:T(128)} %amplitude_ref.1) | copy-start | bytes 388
  33.5 26.3 %all-to-all-start = ((bf16[16,32,512]{2,1,0:T(8,128)(2,1)}), bf16[16,32,512]{2,1,0:T(8,128)(2,1)S(1)}, u32[]{:S(2)}, u32[]{:S(2)}) async-start(bf16[16,32,512]{2,1,0:T(8,128)(2,1)} %get-tuple-element.24), calls=%async_computation | async-start | bytes 1048576 | tf_op jit(solution)/shard_map/all_to_all | solution.py:400
  43.2 11.1 %collective-permute-start.12 = (bf16[32,512]{1,0:T(8,128)(2,1)S(1)}, bf16[32,512]{1,0:T(8,128)(2,1)S(1)}, u32[]{:S(2)}, u32[]{:S(2)}) collective-permute-start(bf16[32,512]{1,0:T(8,128)(2,1)S(1)} %get-tuple-element.25.own_ref), channel_id=1, source_target_pairs={{0,96},{32,64},{128,224},{160,192},{256,352},{288,320},{384,480},{... | collective-permute-start | bytes 98312 | tf_op jit(solution)/shard_map/ppermute | solution.py:403
  48.7 5.6 %collective-permute-start.11 = (bf16[32,512]{1,0:T(8,128)(2,1)S(1)}, bf16[32,512]{1,0:T(8,128)(2,1)S(1)}, u32[]{:S(2)}, u32[]{:S(2)}) collective-permute-start(bf16[32,512]{1,0:T(8,128)(2,1)S(1)} %get-tuple-element.25.own_ref), channel_id=1, source_target_pairs={{0,64},{32,96},{128,192},{160,224},{256,320},{288,352},{384,448},{... | collective-permute-start | bytes 98312 | tf_op jit(solution)/shard_map/ppermute | solution.py:403
  51.8 6.7 %collective-permute-start.10 = (bf16[32,512]{1,0:T(8,128)(2,1)S(1)}, bf16[32,512]{1,0:T(8,128)(2,1)S(1)}, u32[]{:S(2)}, u32[]{:S(2)}) collective-permute-start(bf16[32,512]{1,0:T(8,128)(2,1)S(1)} %get-tuple-element.25.own_ref), channel_id=1, source_target_pairs={{0,32},{32,0},{128,160},{160,128},{256,288},{288,256},{384,416},{4... | collective-permute-start | bytes 98312 | tf_op jit(solution)/shard_map/ppermute | solution.py:403
